TPU v7x, 32 devices: a whole 2x2x4 slice. The times are simulated.
32 devices in a mesh: groups: 2 (over y), vocab: 4 (over z), tok: 2 (over x), sub: 2 (over core).
Axes of the slice: x: 2, y: 2, z: 4, core: 2. Of those that a mesh axis runs over, the one named last changes fastest.
Arguments:
- teacher_logits: bfloat16 [1024, 16384], P(('groups', 'tok', 'sub'), 'vocab'), parts along dimension 0, may hold values from -12 to 340
- student_logits: bfloat16 [1024, 256000], P(('groups', 'tok', 'sub'), 'vocab'), parts along dimension 0, may hold values from -12 to 340
- token_ids: int32 [1024], P(('groups', 'tok', 'sub')), parts along dimension 0, may hold values from 0 to 255999
- align_values: bfloat16 [128, 4096], P('vocab'), may hold values from 0.00049972534 to 0.049804688
- block_rows: int32 [128], P('vocab'), may hold values from 0 to 63
- block_cols: int32 [128], P('vocab'), may hold values from 0 to 999
- block_counts: int32 [4], P('vocab'), may hold values from 4 to 32, as said below
Outputs:
- logit_grad: bfloat16 [1024, 256000], P(('groups', 'tok', 'sub'), 'vocab'), parts along dimension 0
- token_loss: float32 [1024], P(('groups', 'tok', 'sub')), parts along dimension 0
There are 2 independent parts, one for each index of `groups`. A program takes and returns all parts, laid end to end along the dimension named above; an argument that names none is the same for every part. Nothing has to cross between parts.
Inputs may be any that keep to these rules, and one draw needn't show every extreme that they name: Panel p uses its first block_counts[p] slots; later slots are not part of the alignment. Some panel uses all 32.
All inputs are finite; a program needn't handle non-finite values.
Results may differ from a plain program's by a relative error of at most 0.0034.
Values may be sent and summed in bfloat16 or wider, within the bound.
A program may use at most 256 MiB of HBM per device.

v0:
```python
import jax
import jax.numpy as jnp
from jax import lax
from jax.sharding import PartitionSpec as P

BLK = 64
MAXB = 32


def merged(value, axis, join):
    pieces = jax.tree.map(lambda part: lax.all_gather(part, axis), value)
    head = jax.tree.map(lambda part: part[0], pieces)
    tail = jax.tree.map(lambda part: part[1:], pieces)
    total, _ = lax.scan(lambda total, slab: (join(total, slab), None), head, tail)
    return total


def merge_stats(earlier, later):
    joint_top = jnp.maximum(earlier[0], later[0])
    joint_total = earlier[1] * jnp.exp(earlier[0] - joint_top) + later[1] * jnp.exp(
        later[0] - joint_top
    )
    return (joint_top, joint_total)


def local(
    teacher_logits, student_logits, token_ids, align_values, block_rows, block_cols, block_counts
):
    vocab_count = lax.axis_size("vocab")
    tok_rows = teacher_logits.shape[0]
    col_width = student_logits.shape[1]
    col_blocks = col_width // BLK
    row_blocks = teacher_logits.shape[1] // BLK
    per_dest = MAXB // vocab_count
    scores = teacher_logits.astype(jnp.float32)
    local_top = jnp.max(scores, axis=1)
    local_total = jnp.sum(jnp.exp(scores - local_top[:, None]), axis=1)
    row_top, row_total = merged((local_top, local_total), "vocab", merge_stats)
    teacher_probs = (jnp.exp(scores - row_top[:, None]) / row_total[:, None]).astype(jnp.bfloat16)
    live_slots = lax.iota(jnp.int32, MAXB) < block_counts[0]
    flat_blocks = align_values * live_slots[:, None].astype(jnp.bfloat16)
    moved_rows = lax.all_to_all(teacher_probs, "vocab", split_axis=0, concat_axis=1, tiled=True)
    few_rows = tok_rows // vocab_count
    tiled_probs = moved_rows.reshape(few_rows, -1, BLK)
    index_table = lax.all_gather(jnp.stack([block_rows, block_cols]), "vocab", axis=1, tiled=True)
    zero_dense = jnp.zeros((vocab_count * col_blocks, few_rows * BLK), jnp.float32)
    shard_piece = lax.all_gather(flat_blocks, "vocab", axis=0, tiled=True)
    slot_count = shard_piece.shape[0]
    slot_ids = lax.iota(jnp.int32, slot_count)
    owner_ids = slot_ids // MAXB
    dest_ids = slot_ids % MAXB // per_dest
    row_ids = index_table[0] + owner_ids * row_blocks
    col_ids = index_table[1] + dest_ids * col_blocks
    picked_cols = jnp.take(tiled_probs, row_ids, axis=1)
    block_terms = jnp.einsum(
        "rbk,bkc->brc",
        picked_cols,
        shard_piece.reshape(slot_count, BLK, BLK),
        preferred_element_type=jnp.float32,
    )
    dense_target = zero_dense.at[col_ids].add(block_terms.reshape(slot_count, few_rows * BLK))
    target_blocks = lax.all_to_all(
        dense_target.reshape(vocab_count * col_blocks, few_rows, BLK),
        "vocab",
        split_axis=0,
        concat_axis=1,
        tiled=True,
    )
    target = jnp.transpose(target_blocks, (1, 0, 2)).reshape(tok_rows, col_width)
    logits = student_logits.astype(jnp.float32)
    offset = lax.axis_index("vocab") * col_width
    id_hit = lax.iota(jnp.int32, col_width)[None, :] == (token_ids - offset)[:, None]
    part_top = jnp.max(logits, axis=1)
    part_mass = jnp.sum(target, axis=1)
    part_cross = jnp.sum(target * logits, axis=1)
    part_pick = jnp.sum(jnp.where(id_hit, logits, 0.0), axis=1)
    student_top = lax.pmax(part_top, "vocab")
    part_total = jnp.sum(jnp.exp(logits - student_top[:, None]), axis=1)
    student_total, mass, cross, picked = lax.psum(
        (part_total, part_mass, part_cross, part_pick), "vocab"
    )
    log_norm = student_top + jnp.log(student_total)
    weight = mass + 1.0
    token_loss = weight * log_norm - cross - picked
    logit_grad = (
        weight[:, None] * jnp.exp(logits - log_norm[:, None]) - target - id_hit.astype(jnp.float32)
    )
    return (logit_grad.astype(jnp.bfloat16), token_loss)


def solution(mesh):
    return jax.shard_map(
        local,
        mesh=mesh,
        in_specs=(
            P(("groups", "tok", "sub"), "vocab"),
            P(("groups", "tok", "sub"), "vocab"),
            P(("groups", "tok", "sub")),
            P("vocab", None),
            P("vocab"),
            P("vocab"),
            P("vocab"),
        ),
        out_specs=(P(("groups", "tok", "sub"), "vocab"), P(("groups", "tok", "sub"))),
        check_vma=False,
    )
```

profile of v0, /device:TPU:0, one launch (start us, length us, event | category | flops | bytes accessed | tf_op | source)
XLA Modules:
  0.0 1407.1 jit_solution(7885729734571279025)
XLA Ops:
  10.3 12.5 all-gather.4
  22.9 7.5 all-gather.3
  33.2 3.5 all-to-all-start
  39.9 19.3 %all-gather.2 = s32[4,32,2]{1,2,0:T(2,128)S(1)} all-gather(s32[1,32,2]{1,2,0:T(2,128)S(1)} %add_bitcast_fusion), channel_id=1, replica_groups=mesh['groups'=2,'vocab'=4,'tok'=2,'sub'=2] {'vocab'}, dimensions={0}, use_global_device_ids=true | all-gather | bytes 1280 | tf_op jit(solution)/shard_map/all_gather | solution.py:45
  59.3 14.6 %all-to-all-done = bf16[4,32,4096]{2,1,0:T(8,128)(2,1)S(1)} async-done(((bf16[4,32,4096]{2,1,0:T(8,128)(2,1)}), bf16[4,32,4096]{2,1,0:T(8,128)(2,1)S(1)}, u32[]{:S(2)}, u32[]{:S(2)}) %all-to-all-start) | async-done | bytes 1048608 | tf_op jit(solution)/shard_map/all_to_all | solution.py:42
  91.1 15.4 %scatter_custom_fusion = f32[4000,2048]{1,0:T(8,128)} fusion(s32[128]{0:T(128)S(1)} %get-tuple-element.60, f32[128,2048]{1,0:T(8,128)S(1)} %copy.35, f32[]{:T(128)} %constant.71.clone.1), kind=kCustom, calls=%fused_computation.23 | custom fusion | flops 262144 | bytes 32768004 | tf_op jit(solution)/shard_map/scatter-add | solution.py:61
  106.6 30.7 %copy.36 = f32[4000,2048]{0,1:T(8,128)} copy(f32[4000,2048]{1,0:T(8,128)} %scatter_custom_fusion) | data formatting | bytes 65536000 | tf_op jit(solution)/shard_map/scatter-add | solution.py:61
  137.2 58.3 %copy.37 = f32[4000,32,64]{2,1,0:T(8,128)} copy(f32[4000,32,64]{0,2,1:T(8,128)} %bitcast.73) | data formatting | bytes 65536000 | tf_op jit(solution)/shard_map/reshape | solution.py:63
  195.6 83.1 %reshape.238 = f32[4,1,2048000]{2,1,0:T(1,128)} reshape(f32[4000,32,64]{2,1,0:T(8,128)} %copy.37) | data formatting | bytes 65536000
  278.7 9.6 all-to-all-start.1
  288.3 22.1 %copy.40 = bf16[128,64000]{0,1:T(8,128)(2,1)} copy(bf16[128,64000]{1,0:T(8,128)(2,1)} %param.10) | data formatting | bytes 32768000 | tf_op args[1]
  310.4 8.8 reduce_max.36
  319.1 499.8 %pmax.7 = f32[128]{0:T(128)S(1)} all-reduce(bf16[128]{0:T(256)(128)(2,1)S(1)} %reduce_max.36), channel_id=1, replica_groups=mesh['groups'=2,'vocab'=4,'tok'=2,'sub'=2] {'vocab'}, use_global_device_ids=true, to_apply=%region_8.9 | all-reduce | flops 128 | bytes 768 | tf_op jit(solution)/shard_map/pmax | solution.py:77
  819.0 172.7 %all-to-all-done.1 = f32[4,1,2048000]{2,1,0:T(1,128)} async-done(((f32[4,1,2048000]{2,1,0:T(1,128)}), f32[4,1,2048000]{2,1,0:T(1,128)}, u32[]{:S(2)}, u32[]{:S(2)}) %all-to-all-start.1) | async-done | bytes 32768032 | tf_op jit(solution)/shard_map/all_to_all | solution.py:62
  992.2 99.0 %reduce.5 = f32[4,2048000]{1,0:T(4,128)} reduce(f32[4,1,2048000]{2,1,0:T(1,128)} %all-to-all-done.1, f32[]{:T(128)} %broadcast.216), dimensions={1}, to_apply=%all_to_all.28.reduce_sub_computation | reduce | bytes 65536004 | tf_op jit(solution)/shard_map/all_to_all | solution.py:62
  1091.2 104.9 %reshape.239 = f32[4000,32,64]{2,1,0:T(8,128)} reshape(f32[4,2048000]{1,0:T(4,128)} %reduce.5) | data formatting | bytes 65536000
  1196.0 49.0 %copy.44 = f32[4,1000,32,64]{1,0,3,2:T(4,128)} copy(f32[4,1000,32,64]{3,2,1,0:T(8,128)} %bitcast.72) | data formatting | bytes 65536000 | tf_op jit(solution)/shard_map/all_to_all | solution.py:62
  1245.0 11.9 bitcast_reduce_fusion
  1256.9 32.0 %copy.41 = f32[1000,4,32,64]{0,3,2,1:T(8,128)} copy(f32[1000,4,32,64]{0,1,3,2:T(4,128)} %bitcast.71) | data formatting | bytes 65536000 | tf_op jit(solution)/shard_map/all_to_all | solution.py:62
  1288.8 32.5 %copy.42 = f32[128,1000,64]{0,2,1:T(8,128)} copy(f32[128,1000,64]{1,2,0:T(8,128)} %bitcast.74) | data formatting | bytes 65536000 | tf_op jit(solution)/shard_map/transpose | solution.py:69
  1321.5 19.4 %fusion.12 = (f32[128]{0:T(128)S(1)}, f32[128]{0:T(128)S(1)}, f32[128]{0:T(128)S(1)}) fusion(bf16[128,64000]{0,1:T(8,128)(2,1)} %copy.40, f32[128,1000,64]{0,2,1:T(8,128)} %copy.42, s32[128]{0:T(128)S(1)} %broadcast_subtract_fusion, f32[128]{0:T(128)S(1)} %pmax.7), kind=kLoop, calls=%fused_computation.20 | loop fusion | flops 65535616 | bytes 49154560 | tf_op jit(solution)/shard_map/reduce_sum | solution.py:75
  1340.9 11.9 all-reduce
  1353.3 24.7 %fusion.11 = bf16[128,64000]{0,1:T(8,128)(2,1)} fusion(bf16[128,64000]{0,1:T(8,128)(2,1)} %copy.40, f32[128,1000,64]{0,2,1:T(8,128)} %copy.42, s32[128]{0:T(128)S(1)} %broadcast_subtract_fusion, f32[128]{0:T(128)S(1)} %get-tuple-element.58, f32[128]{0:T(128)S(1)} %get-tuple-element.61), kind=kLoop, calls=%fused_computation.19 | loop fusion | flops 65536000 | bytes 65537536 | tf_op jit(solution)/shard_map/convert_element_type | solution.py:88
  1378.0 22.1 %copy.43 = bf16[128,64000]{1,0:T(8,128)(2,1)} copy(bf16[128,64000]{0,1:T(8,128)(2,1)} %fusion.11) | data formatting | bytes 32768000
  (41 shorter events, 27.0 us)
Async XLA Ops:
  33.2 40.8 %all-to-all-start = ((bf16[4,32,4096]{2,1,0:T(8,128)(2,1)}), bf16[4,32,4096]{2,1,0:T(8,128)(2,1)S(1)}, u32[]{:S(2)}, u32[]{:S(2)}) async-start(bf16[4,32,4096]{2,1,0:T(8,128)(2,1)} %bitcast.14), calls=%async_computation | async-start | bytes 2097152 | tf_op jit(solution)/shard_map/all_to_all | solution.py:42
  36.7 42.4 %all-gather.7.cloned.1.call-start = ((), (), s32[]{:S(2)}) async-start(), calls=%async_computation.2 | async-start | bytes 1310720 | tf_op jit(solution)/shard_map/all_gather | solution.py:47
  278.7 713.0 %all-to-all-start.1 = ((f32[4,1,2048000]{2,1,0:T(1,128)}), f32[4,1,2048000]{2,1,0:T(1,128)}, u32[]{:S(2)}, u32[]{:S(2)}) async-start(f32[4,1,2048000]{2,1,0:T(1,128)} %reshape.238), calls=%async_computation.1 | async-start | bytes 65536000 | tf_op jit(solution)/shard_map/all_to_all | solution.py:62
  288.3 530.7 %copy-start = (s32[128]{0:T(128)S(1)}, s32[128]{0:T(128)}, u32[]{:S(2)}) copy-start(s32[128]{0:T(128)} %param.11) | copy-start | bytes 1540
Sparse Core Ops, SparseCore 0:
  39.3 36.8 all-gather.6
where the time goes:
time: 1420 us; the launch traced here: 1410 us
  blocking collectives  551 us (39%)
  local copies, waits for them, and re-layouts  450 us (32%)
  other arithmetic  188 us (13%)
  waiting for transfers between devices  187 us (13%)
  between operations  15 us (1%)
    pmax x1, blocking collectives, local(): student_top = lax.pmax(part_top, 'vocab')  500 us
    unnamed x9, local copies, waits for them, and re-layouts  232 us
    all_to_all x1, waiting for transfers between devices, local(): lax.all_to_all(dense_target.reshape(vocab_count * col_blocks, few_rows, B...  173 us
    all_to_all x1, other arithmetic, local(): lax.all_to_all(dense_target.reshape(vocab_count * col_blocks, few_rows, B...  99 us
    all_to_all x3, local copies, waits for them, and re-layouts, local(): lax.all_to_all(dense_target.reshape(vocab_count * col_blocks, few_rows, B...  81.4 us
    reshape x1, local copies, waits for them, and re-layouts, local(): dense_target.reshape(vocab_count * col_blocks, few_rows, BLK)  58.3 us
    transpose x1, local copies, waits for them, and re-layouts, local(): jnp.transpose(target_blocks, (1, 0, 2)).reshape(tok_rows, col_width)  32.5 us
    scatter-add x1, local copies, waits for them, and re-layouts, local(): zero_dense.at[col_ids].add(block_terms.reshape(slot_count, few_rows * BLK))  30.7 us
  transfers between devices with their start and end apart: 3, of which 2 were waited for; matrix products, arithmetic and copies ran while one was open for 3% of the time, Pallas kernels for 0%

commit v1 on v0

v1 whole, which is shorter than its diff:
```python
import functools

import jax
import jax.numpy as jnp
from jax import lax
from jax.experimental import pallas as pl
from jax.experimental.pallas import tpu as pltpu
from jax.sharding import PartitionSpec as P

BLK = 64
MAXB = 32
LANES = 128
ROWS = 16
CHUNK = 1280
VMEM = pltpu.VMEM
SMEM = pltpu.SMEM
LIMIT = 40 * 1024 * 1024


def lane_tile(index):
    return pl.ds(pl.multiple_of(index * LANES, LANES), LANES)


def fold(value, join):
    parts = [value[:, k : k + LANES] for k in range(0, value.shape[1], LANES)]
    while len(parts) > 1:
        parts = [join(*parts[k : k + 2]) if k + 1 < len(parts) else parts[k] for k in range(0, len(parts), 2)]
    return parts[0]


def pick_kernel(rows_ref, logits_ref, top_ref, total_ref, picks_ref):
    top = top_ref[...]
    total = total_ref[...]

    def body(slot, _):
        row = rows_ref[slot]
        scores = logits_ref[:, lane_tile(row // 2)].astype(jnp.float32)
        probs = jnp.transpose(jnp.exp(scores - top) / total)
        picks_ref[slot] = jnp.where(row % 2 == 0, probs[:BLK], probs[BLK:]).astype(jnp.bfloat16)
        return _

    lax.fori_loop(0, MAXB, body, 0, unroll=4)


def stats_kernel(width, tile_ref, ids_ref, logits_ref, top_ref, total_ref, picked_ref, seen_ref):
    step = pl.program_id(0)
    whole = width // CHUNK
    tail = logits_ref.shape[1] - whole * CHUNK

    def chunk(index):
        return logits_ref[:, pl.ds(pl.multiple_of(index * CHUNK, CHUNK), CHUNK)]

    def max_body(index, top):
        return jnp.maximum(top, fold(chunk(index), jnp.maximum))

    top = lax.fori_loop(
        0, whole, max_body, jnp.full((ROWS, LANES), -jnp.inf, jnp.bfloat16), unroll=2
    ).astype(jnp.float32)
    if tail:
        rest = logits_ref[:, whole * CHUNK :].astype(jnp.float32)
        live = lax.broadcasted_iota(jnp.int32, rest.shape, 1) < width - whole * CHUNK
        top = jnp.maximum(top, fold(jnp.where(live, rest, -jnp.inf), jnp.maximum))
    top = jnp.max(top, axis=1, keepdims=True)

    def sum_body(index, total):
        return total + fold(jnp.exp(chunk(index).astype(jnp.float32) - top), jnp.add)

    total = lax.fori_loop(0, whole, sum_body, jnp.zeros((ROWS, LANES), jnp.float32), unroll=2)
    if tail:
        total = total + fold(jnp.where(live, jnp.exp(rest - top), 0.0), jnp.add)
    top_ref[...] = top
    total_ref[...] = jnp.sum(total, axis=1, keepdims=True)

    row_iota = lax.broadcasted_iota(jnp.int32, (ROWS, LANES), 0)
    lane_iota = lax.broadcasted_iota(jnp.int32, (ROWS, LANES), 1)
    picked = jnp.zeros((ROWS, LANES), jnp.float32)
    for row in range(ROWS):
        place = ids_ref[step * ROWS + row]
        tile = jnp.clip(place, 0, width - 1) // LANES
        here = logits_ref[:, lane_tile(tile)].astype(jnp.float32)
        hit = (row_iota == row) & (lane_iota == place - tile * LANES)
        picked = jnp.where(hit, here, picked)
    picked_ref[...] = jnp.sum(picked, axis=1, keepdims=True)
    for slot in range(MAXB):
        seen_ref[slot] = logits_ref[:, lane_tile(tile_ref[slot])]


def target_kernel(half_ref, first_ref, picks_ref, blocks_ref, seen_ref, target_ref, mass_ref, cross_ref):
    target_ref[...] = jnp.zeros_like(target_ref)
    rows = target_ref.shape[1]
    side = lax.broadcasted_iota(jnp.int32, (1, LANES), 1) // BLK

    def body(slot, carry):
        mass, cross = carry
        here = side == half_ref[slot]
        block = jnp.where(here, blocks_ref[slot].astype(jnp.float32), 0.0).astype(jnp.bfloat16)
        term = lax.dot_general(
            picks_ref[slot], block, (((0,), (0,)), ((), ())), preferred_element_type=jnp.float32
        )
        first = first_ref[slot]
        target_ref[first] = target_ref[first] + term
        return mass + term, cross + jnp.where(here, term * seen_ref[slot].astype(jnp.float32), 0.0)

    zero = jnp.zeros((rows, LANES), jnp.float32)
    mass, cross = lax.fori_loop(0, MAXB, body, (zero, zero), unroll=2)
    mass_ref[...] = jnp.sum(mass, axis=1, keepdims=True)
    cross_ref[...] = jnp.sum(cross, axis=1, keepdims=True)


def grad_kernel(tile_ref, first_ref, ids_ref, shift_ref, target_ref, logits_ref, grad_ref):
    width = logits_ref.shape[1]
    shift = shift_ref[...]
    ids = ids_ref[...]

    def part(start, size):
        scores = logits_ref[:, pl.ds(start, size)].astype(jnp.float32)
        hit = lax.broadcasted_iota(jnp.int32, (ROWS, size), 1) == ids - start
        return jnp.exp(scores - shift) - jnp.where(hit, 1.0, 0.0)

    def body(index, _):
        start = pl.multiple_of(index * CHUNK, CHUNK)
        grad_ref[:, pl.ds(start, CHUNK)] = part(start, CHUNK).astype(jnp.bfloat16)
        return _

    whole = width // CHUNK
    lax.fori_loop(0, whole, body, 0, unroll=2)
    if width % CHUNK:
        start = whole * CHUNK
        grad_ref[:, pl.ds(start, width - start)] = part(start, width - start).astype(jnp.bfloat16)
    for slot in range(MAXB):
        start = pl.multiple_of(tile_ref[slot] * LANES, LANES)
        grad = part(start, LANES) - target_ref[first_ref[slot]]
        grad_ref[:, pl.ds(start, LANES)] = grad.astype(jnp.bfloat16)


def params():
    return pltpu.CompilerParams(vmem_limit_bytes=LIMIT)


def local(
    teacher_logits, student_logits, token_ids, align_values, block_rows, block_cols, block_counts
):
    count = lax.axis_size("vocab")
    me = lax.axis_index("vocab")
    rows = teacher_logits.shape[0]
    width = student_logits.shape[1]
    padded = pl.cdiv(width, LANES) * LANES
    per_dest = MAXB // count
    steps = rows // ROWS
    smem = pl.BlockSpec(memory_space=SMEM)
    vmem = pl.BlockSpec(memory_space=VMEM)
    f32 = lambda *shape: jax.ShapeDtypeStruct(shape, jnp.float32)
    b16 = lambda *shape: jax.ShapeDtypeStruct(shape, jnp.bfloat16)

    live = lax.iota(jnp.int32, MAXB) < block_counts[0]
    sent_blocks = jnp.where(live[:, None], align_values, jnp.zeros_like(align_values))
    blocks = lax.all_to_all(sent_blocks, "vocab", split_axis=0, concat_axis=0, tiled=True)

    scores = teacher_logits.astype(jnp.float32)
    part_top = jnp.max(scores, axis=1)
    part_total = jnp.sum(jnp.exp(scores - part_top[:, None]), axis=1)
    parts = lax.all_gather(
        jnp.concatenate([part_top, part_total, block_cols.astype(jnp.float32)]), "vocab"
    )
    tops, totals = parts[:, :rows], parts[:, rows : 2 * rows]
    top = jnp.max(tops, axis=0)
    total = jnp.sum(totals * jnp.exp(tops - top), axis=0)
    cols = parts[:, 2 * rows :].astype(jnp.int32).reshape(count, count, per_dest)
    cols = lax.dynamic_index_in_dim(cols, me, 1, keepdims=False).reshape(MAXB)
    tile, half = cols // 2, cols % 2
    first = jnp.argmax(tile[:, None] == tile[None, :], axis=1).astype(jnp.int32)

    picks = pl.pallas_call(
        pick_kernel,
        out_shape=b16(MAXB, BLK, rows),
        in_specs=[smem, vmem, vmem, vmem],
        out_specs=vmem,
        compiler_params=params(),
    )(block_rows, teacher_logits, top[:, None], total[:, None])
    picks = lax.all_to_all(picks, "vocab", split_axis=0, concat_axis=0, tiled=True)

    ids = token_ids - me * width
    row_spec = pl.BlockSpec((ROWS, 1), lambda i: (i, 0))
    wide_spec = pl.BlockSpec((ROWS, padded), lambda i: (i, 0))
    slot_spec = pl.BlockSpec((MAXB, ROWS, LANES), lambda i: (0, i, 0))
    size = rows * width
    student_top, student_total, picked, seen = pl.pallas_call(
        functools.partial(stats_kernel, width),
        out_shape=(f32(rows, 1), f32(rows, 1), f32(rows, 1), b16(MAXB, rows, LANES)),
        grid=(steps,),
        in_specs=[smem, smem, wide_spec],
        out_specs=(row_spec, row_spec, row_spec, slot_spec),
        compiler_params=params(),
        cost_estimate=pl.CostEstimate(flops=8 * size, bytes_accessed=2 * size, transcendentals=size),
    )(tile, ids, student_logits)

    blocks = blocks.reshape(MAXB, BLK, BLK)
    blocks = jnp.concatenate([blocks, blocks], axis=2)
    target, mass, cross = pl.pallas_call(
        target_kernel,
        out_shape=(f32(MAXB, rows, LANES), f32(rows, 1), f32(rows, 1)),
        in_specs=[smem, smem, vmem, vmem, vmem],
        out_specs=(vmem, vmem, vmem),
        compiler_params=params(),
    )(half, first, picks, blocks, seen)

    sums = jnp.concatenate([student_top, student_total, mass, cross, picked], axis=1).T
    sums = lax.all_gather(sums, "vocab")
    top = jnp.max(sums[:, 0], axis=0)
    total = jnp.sum(sums[:, 1] * jnp.exp(sums[:, 0] - top), axis=0)
    mass, cross, picked = jnp.sum(sums[:, 2:], axis=0)
    log_norm = top + jnp.log(total)
    weight = mass + 1.0
    token_loss = weight * log_norm - cross - picked
    shift = log_norm - jnp.log(weight)

    logit_grad = pl.pallas_call(
        grad_kernel,
        out_shape=b16(rows, width),
        grid=(steps,),
        in_specs=[smem, smem, row_spec, row_spec, slot_spec, wide_spec],
        out_specs=wide_spec,
        compiler_params=params(),
        cost_estimate=pl.CostEstimate(flops=8 * size, bytes_accessed=4 * size, transcendentals=size),
    )(tile, first, ids[:, None], shift[:, None], target, student_logits)
    return logit_grad, token_loss


def solution(mesh):
    return jax.shard_map(
        local,
        mesh=mesh,
        in_specs=(
            P(("groups", "tok", "sub"), "vocab"),
            P(("groups", "tok", "sub"), "vocab"),
            P(("groups", "tok", "sub")),
            P("vocab", None),
            P("vocab"),
            P("vocab"),
            P("vocab"),
        ),
        out_specs=(P(("groups", "tok", "sub"), "vocab"), P(("groups", "tok", "sub"))),
        check_vma=False,
    )
```

time: 1420 us -> 99 us (0.07)
  blocking collectives: 551 us -> 26 us
  local copies, waits for them, and re-layouts: 450 us -> 4.57 us
  waiting for transfers between devices: 187 us -> 0.01 us
  other arithmetic: 188 us -> 6.29 us
  Pallas kernels: 0 us -> 49.6 us
    pmax x1 -> x0, blocking collectives: 500 us -> none  [local(): student_top = lax.pmax(part_top, 'vocab')]
    unnamed x9 -> x15, local copies, waits for them, and re-layouts: 232 us -> 2.91 us
    all_to_all x2, waiting for transfers between devices: 187 us -> 0.01 us  [the longest x1 0.01 us: local(): lax.all_to_all(sent_blocks, 'vocab', split_axis=0, concat_axis=0, tiled=T...]
    all_to_all x1, other arithmetic: 99 us -> 1.74 us  [local(): lax.all_to_all(sent_blocks, 'vocab', split_axis=0, concat_axis=0, tiled=T...]
    all_to_all x4 -> x0, local copies, waits for them, and re-layouts: 82.2 us -> none  [the longest x3 81.4 us: local(): lax.all_to_all(dense_target.reshape(vocab_count * col_blocks, few_rows, B...]
    reshape x5 -> x3, local copies, waits for them, and re-layouts: 65.9 us -> 0.71 us  [the longest x1 0.54 us: local(): blocks = blocks.reshape(MAXB, BLK, BLK)]
    pallas_call x0 -> x4, Pallas kernels: none -> 49.6 us  [the longest x1 26.8 us: local(): pl.pallas_call(grad_kernel, out_shape=b16(rows, width), grid=(steps,), in...]
    transpose x1 -> x0, local copies, waits for them, and re-layouts: 32.5 us -> none  [local(): jnp.transpose(target_blocks, (1, 0, 2)).reshape(tok_rows, col_width)]
  transfers between devices with their start and end apart: 3 -> 2, of which waited for: 2 -> 0; matrix products, arithmetic and copies ran while one was open for 3% -> 6% of each run, Pallas kernels for 0% -> 19%
where the time goes in v1:
time: 99 us; the launch traced here: 98.4 us
  Pallas kernels  49.6 us (50%)
  blocking collectives  26 us (26%)
  starting transfers between devices  9.79 us (10%)
  other arithmetic  6.29 us (6%)
  local copies, waits for them, and re-layouts  4.57 us (5%)
  between operations  2.2 us (2%)
    pallas_call x1, Pallas kernels, local(): pl.pallas_call(grad_kernel, out_shape=b16(rows, width), grid=(steps,), in...  26.8 us
    pallas_call x1, Pallas kernels, local(): pl.pallas_call(functools.partial(stats_kernel, width), out_shape=(f32(row...  14.5 us
    all_gather x1, blocking collectives, local(): sums = lax.all_gather(sums, 'vocab')  13.7 us
    unnamed x1, blocking collectives  12.3 us
    all_to_all x1, starting transfers between devices, local(): lax.all_to_all(sent_blocks, 'vocab', split_axis=0, concat_axis=0, tiled=T...  6.32 us
    pallas_call x1, Pallas kernels, local(): pl.pallas_call(pick_kernel, out_shape=b16(MAXB, BLK, rows), in_specs=[sme...  4.26 us
    pallas_call x1, Pallas kernels, local(): pl.pallas_call(target_kernel, out_shape=(f32(MAXB, rows, LANES), f32(rows...  4.14 us
    all_to_all x1, starting transfers between devices, local(): lax.all_to_all(picks, 'vocab', split_axis=0, concat_axis=0, tiled=True)  3.47 us
  transfers between devices with their start and end apart: 2, of which 0 were waited for; matrix products, arithmetic and copies ran while one was open for 6% of the time, Pallas kernels for 19%

profile of v1, /device:TPU:0, one launch (start us, length us, event | category | flops | bytes accessed | tf_op | source)
XLA Modules:
  0.0 98.4 jit_solution(16086981333512529341)
XLA Ops:
  1.4 1.7 %select_bitcast_fusion = bf16[4,8,4096]{2,1,0:T(8,128)(2,1)} fusion(bf16[32,4096]{1,0:T(8,128)(2,1)} %param.10, pred[32]{0:T(512)(128)(4,1)S(1)} %iota_compare_fusion), kind=kLoop, calls=%fused_computation.2 | loop fusion | flops 131072 | bytes 524320 | tf_op jit(solution)/shard_map/all_to_all | solution.py:157
  3.2 6.3 %all-to-all-start.1 = ((bf16[4,8,4096]{2,1,0:T(8,128)(2,1)}), bf16[4,8,4096]{2,1,0:T(8,128)(2,1)S(1)}, u32[]{:S(2)}, u32[]{:S(2)}) async-start(bf16[4,8,4096]{2,1,0:T(8,128)(2,1)} %select_bitcast_fusion), calls=%async_computation.1 | async-start | bytes 524288 | tf_op jit(solution)/shard_map/all_to_all | solution.py:157
  9.5 0.7 convert_element_type.10
  10.1 1.4 %reduce_max.32 = bf16[128]{0:T(256)(128)(2,1)S(1)} reduce(bf16[128,4096]{1,0:T(8,128)(2,1)} %logits_ref.4, bf16[]{:T(256)} %constant.39.clone.1), dimensions={1}, to_apply=%region_0.1 | reduce | flops 524160 | bytes 1048834 | tf_op jit(solution)/shard_map/reduce_max | solution.py:160
  11.6 0.5 exponential_reduce_fusion
  12.1 0.6 dynamic-slice
  13.4 0.1 maximum_dynamic-update-slice_fusion
  13.5 12.3 %all-reduce = f32[1152]{0:T(1024)S(1)} all-reduce(f32[1152]{0:T(1024)S(1)} %maximum_dynamic-update-slice_fusion), channel_id=2, replica_groups=mesh['groups'=2,'vocab'=4,'tok'=2,'sub'=2] {'vocab'}, use_global_device_ids=true, to_apply=%add | all-reduce | flops 1152 | bytes 9216
  26.1 0.1 copy.59.total_ref
  26.5 4.3 %shard_map.87 = bf16[32,64,128]{2,1,0:T(8,128)(2,1)} custom-call(s32[32]{0:T(128)S(1)} %copy-done.3, bf16[128,4096]{1,0:T(8,128)(2,1)S(1)} %copy-done, f32[128,1]{1,0:T(8,128)S(1)} %copy.58.top_ref, f32[128,1]{1,0:T(8,128)S(1)} %copy.59.total_ref), custom_call_target="tpu_custom_call" | custom-call | tf_op jit(solution)/shard_map/pallas_call | solution.py:173
  30.8 3.5 %all-to-all-start = ((bf16[32,64,128]{2,1,0:T(8,128)(2,1)}), bf16[32,64,128]{2,1,0:T(8,128)(2,1)S(1)}, u32[]{:S(2)}, u32[]{:S(2)}) async-start(bf16[32,64,128]{2,1,0:T(8,128)(2,1)} %shard_map.87), calls=%async_computation | async-start | bytes 1048576 | tf_op jit(solution)/shard_map/all_to_all | solution.py:180
  34.3 14.5 %shard_map.86 = (f32[128,1]{1,0:T(8,128)S(1)}, f32[128,1]{1,0:T(8,128)S(1)}, f32[128,1]{1,0:T(8,128)S(1)}, bf16[32,128,128]{2,1,0:T(8,128)(2,1)S(1)}) custom-call(s32[32]{0:T(128)S(1)} %get-tuple-element.24.tile_ref, s32[128]{0:T(128)S(1)} %broadcast_subtract_fusion.ids_ref, bf16[128,64000]{1,0:T(8,128)(2,1)} %logits_ref.5), custom_call_target="tpu_custom_call" | custom-call | flops 65536000 | bytes 16384000 | tf_op jit(solution)/shard_map/pallas_call | solution.py:187
  48.8 1.0 copy-done.1
  49.9 0.7 iota_reduce_fusion
  50.7 0.5 reshape.121
  51.2 0.3 pad_maximum_fusion.blocks_ref
  51.5 1.2 %copy-done.2 = bf16[32,128,128]{2,1,0:T(8,128)(2,1)S(1)} copy-done((bf16[32,128,128]{2,1,0:T(8,128)(2,1)S(1)}, bf16[32,128,128]{2,1,0:T(8,128)(2,1)}, u32[]{:S(2)}) %copy-start.2) | copy-done | bytes 1048600
  52.7 4.1 %shard_map.88 = (f32[32,128,128]{2,1,0:T(8,128)S(1)}, f32[128,1]{1,0:T(8,128)S(1)}, f32[128,1]{1,0:T(8,128)S(1)}) custom-call(s32[32]{0:T(128)S(1)} %get-tuple-element.23.half_ref, s32[32]{0:T(128)S(1)} %get-tuple-element.10.first_ref, bf16[32,64,128]{2,1,0:T(8,128)(2,1)S(1)} %all-to-all-done.picks_ref, bf16[32,64,128]{2,1,0:T(8,128)(2,1)S(1)} %pad_maximum_fusion.blocks_ref, ...), custom_call_target="tpu_custom_call" | custom-call | tf_op jit(solution)/shard_map/pallas_call | solution.py:199
  57.1 13.7 %all-gather.2 = f32[4,5,128]{2,1,0:T(8,128)S(1)} all-gather(f32[1,5,128]{2,1,0:T(8,128)S(1)} %bitcast.24), channel_id=3, replica_groups=mesh['groups'=2,'vocab'=4,'tok'=2,'sub'=2] {'vocab'}, dimensions={0}, use_global_device_ids=true | all-gather | bytes 12800 | tf_op jit(solution)/shard_map/all_gather | solution.py:208
  70.8 0.1 copy.69
  70.9 0.1 add_reduce_fusion
  71.0 0.5 bitcast_subtract_fusion
  71.6 0.1 copy.67.shift_ref
  71.7 26.8 %shard_map.89 = bf16[128,64000]{1,0:T(8,128)(2,1)} custom-call(s32[32]{0:T(128)S(1)} %get-tuple-element.24.tile_ref, s32[32]{0:T(128)S(1)} %get-tuple-element.10.first_ref, s32[128,1]{1,0:T(8,128)S(1)} %copy.66.ids_ref, f32[128,1]{1,0:T(8,128)S(1)} %copy.67.shift_ref, f32[32,128,128]{2,1,0:T(8,128)S(1)} %get-tuple-element.17.target_ref, ...), custom_call_target="tpu_custom_call" | custom-call | flops 65536000 | bytes 32768000 | tf_op jit(solution)/shard_map/pallas_call | solution.py:217
  (38 shorter events, 1.1 us)
Async XLA Ops:
  0.6 11.5 %copy-start.5 = (u32[32]{0:T(128)S(1)}, u32[32]{0:T(128)}, u32[]{:S(2)}) copy-start(u32[32]{0:T(128)} %constant.56) | copy-start | bytes 388
  0.6 11.0 %copy-start = (bf16[128,4096]{1,0:T(8,128)(2,1)S(1)}, bf16[128,4096]{1,0:T(8,128)(2,1)}, u32[]{:S(2)}) copy-start(bf16[128,4096]{1,0:T(8,128)(2,1)} %logits_ref.4) | copy-start | bytes 3145732
  0.7 25.6 %copy-start.4 = (s32[128]{0:T(128)S(1)}, s32[128]{0:T(128)}, u32[]{:S(2)}) copy-start(s32[128]{0:T(128)} %param.9) | copy-start | bytes 1540
  0.7 25.8 %copy-start.3 = (s32[32]{0:T(128)S(1)}, s32[32]{0:T(128)}, u32[]{:S(2)}) copy-start(s32[32]{0:T(128)} %rows_ref.1) | copy-start | bytes 388
  3.2 27.6 %all-to-all-start.1 = ((bf16[4,8,4096]{2,1,0:T(8,128)(2,1)}), bf16[4,8,4096]{2,1,0:T(8,128)(2,1)S(1)}, u32[]{:S(2)}, u32[]{:S(2)}) async-start(bf16[4,8,4096]{2,1,0:T(8,128)(2,1)} %select_bitcast_fusion), calls=%async_computation.1 | async-start | bytes 524288 | tf_op jit(solution)/shard_map/all_to_all | solution.py:157
  30.8 20.7 %all-to-all-start = ((bf16[32,64,128]{2,1,0:T(8,128)(2,1)}), bf16[32,64,128]{2,1,0:T(8,128)(2,1)S(1)}, u32[]{:S(2)}, u32[]{:S(2)}) async-start(bf16[32,64,128]{2,1,0:T(8,128)(2,1)} %shard_map.87), calls=%async_computation | async-start | bytes 1048576 | tf_op jit(solution)/shard_map/all_to_all | solution.py:180
  48.7 1.0 copy-start.1
  51.5 1.2 %copy-start.2 = (bf16[32,128,128]{2,1,0:T(8,128)(2,1)S(1)}, bf16[32,128,128]{2,1,0:T(8,128)(2,1)}, u32[]{:S(2)}) copy-start(bf16[32,128,128]{2,1,0:T(8,128)(2,1)} %copy-done.1) | copy-start | bytes 3145732

commit v2 on v1

v2 whole, which is shorter than its diff:
```python
import functools

import jax
import jax.numpy as jnp
from jax import lax
from jax.experimental import pallas as pl
from jax.experimental.pallas import tpu as pltpu
from jax.sharding import PartitionSpec as P

BLK = 64
MAXB = 32
LANES = 128
ROWS = 16
CHUNK = 2560
VMEM = pltpu.VMEM
SMEM = pltpu.SMEM
LIMIT = 40 * 1024 * 1024


def lane_tile(index):
    return pl.ds(pl.multiple_of(index * LANES, LANES), LANES)


def fold(value, join):
    parts = [value[:, k : k + LANES] for k in range(0, value.shape[1], LANES)]
    while len(parts) > 1:
        parts = [join(*parts[k : k + 2]) if k + 1 < len(parts) else parts[k] for k in range(0, len(parts), 2)]
    return parts[0]


def row_stats(load, width):
    whole, tail = divmod(width, CHUNK)

    def chunk(index):
        return load(pl.multiple_of(index * CHUNK, CHUNK), CHUNK)

    def max_body(index, top):
        return jnp.maximum(top, fold(chunk(index), jnp.maximum))

    top = jnp.full((ROWS, LANES), -jnp.inf, jnp.bfloat16)
    top = lax.fori_loop(0, whole, max_body, top).astype(jnp.float32)
    top = jnp.max(top, axis=1, keepdims=True)
    if tail:
        rest = load(whole * CHUNK, tail).astype(jnp.float32)
        top = jnp.maximum(top, jnp.max(rest, axis=1, keepdims=True))

    def sum_body(index, total):
        return total + fold(jnp.exp(chunk(index).astype(jnp.float32) - top), jnp.add)

    total = lax.fori_loop(0, whole, sum_body, jnp.zeros((ROWS, LANES), jnp.float32))
    total = jnp.sum(total, axis=1, keepdims=True)
    if tail:
        total = total + jnp.sum(jnp.exp(rest - top), axis=1, keepdims=True)
    return top, total


def greet(others):
    barrier = pltpu.get_barrier_semaphore()
    for other in others:
        pl.semaphore_signal(
            barrier, inc=1, device_id={"vocab": other}, device_id_type=pl.DeviceIdType.MESH
        )
    return barrier


def remote(source, target, send_sem, recv_sem, other):
    return pltpu.make_async_remote_copy(
        src_ref=source,
        dst_ref=target,
        send_sem=send_sem,
        recv_sem=recv_sem,
        device_id={"vocab": other},
        device_id_type=pl.DeviceIdType.MESH,
    )


def rows_of(index):
    return pl.ds(pl.multiple_of(index * ROWS, ROWS), ROWS)


def spread(part):
    return jnp.broadcast_to(part, (part.shape[0], LANES))


def teacher_kernel(
    count, cols_ref, teacher_ref, stats_ref, all_cols_ref,
    top_at, total_at, own_stats, stats, cols, send_sem, recv_sem,
):
    me = lax.axis_index("vocab")
    others = [lax.rem(me + step, count) for step in range(1, count)]
    barrier = greet(others)

    def body(index, _):
        here = rows_of(index)
        top, total = row_stats(lambda start, size: teacher_ref[here, pl.ds(start, size)], teacher_ref.shape[1])
        top_at[here, :] = spread(top)
        total_at[here, :] = spread(total)
        return _

    lax.fori_loop(0, teacher_ref.shape[0] // ROWS, body, 0)
    sub_iota = lax.broadcasted_iota(jnp.int32, (8, LANES), 0)
    own_stats[...] = jnp.where(
        sub_iota == 0, jnp.transpose(top_at[...])[:8], jnp.transpose(total_at[...])[:8]
    )
    stats[me] = own_stats[...]
    cols[me] = cols_ref[...]
    pl.semaphore_wait(barrier, count - 1)
    copies = []
    for step, other in enumerate(others):
        copies.append(remote(own_stats, stats.at[me], send_sem.at[0, step], recv_sem.at[0, me], other))
        copies.append(remote(cols_ref, cols.at[me], send_sem.at[1, step], recv_sem.at[1, me], other))
    for copy in copies:
        copy.start()
    for step, other in enumerate(others):
        remote(own_stats, stats.at[other], send_sem.at[0, step], recv_sem.at[0, other], other).wait_recv()
        remote(cols_ref, cols.at[other], send_sem.at[1, step], recv_sem.at[1, other], other).wait_recv()
    tops = [stats[index, 0:1] for index in range(count)]
    totals = [stats[index, 1:2] for index in range(count)]
    top = functools.reduce(jnp.maximum, tops)
    total = sum(part * jnp.exp(peak - top) for part, peak in zip(totals, tops))
    stats_ref[...] = jnp.where(sub_iota == 0, top, total)
    all_cols_ref[...] = cols[...]
    for copy in copies:
        copy.wait_send()


def pick_kernel(
    rows_ref, tile_ref, ids_ref, place_ref, teacher_ref, stats_ref, student_ref,
    picks_ref, seen_ref, picked_ref, near, seen_sem, near_sem,
):
    tokens = teacher_ref.shape[0]

    def near_copy(token):
        return pltpu.make_async_copy(
            student_ref.at[rows_of(token // ROWS), lane_tile(place_ref[token])],
            near.at[token],
            near_sem.at[token],
        )

    def seen_copy(slot):
        return pltpu.make_async_copy(
            student_ref.at[:, lane_tile(tile_ref[slot])], seen_ref.at[slot], seen_sem.at[slot]
        )

    def start_near(token, _):
        near_copy(token).start()
        return _

    def start_seen(slot, _):
        seen_copy(slot).start()
        return _

    lax.fori_loop(0, tokens, start_near, 0, unroll=8)
    lax.fori_loop(0, MAXB, start_seen, 0, unroll=8)
    top = stats_ref[0:1]
    total = stats_ref[1:2]

    def body(slot, _):
        row = rows_ref[slot]
        scores = jnp.transpose(teacher_ref[:, lane_tile(row // 2)].astype(jnp.float32))
        scores = jnp.where(row % 2 == 0, scores[:BLK], scores[BLK:])
        picks_ref[slot] = (jnp.exp(scores - top) / total).astype(jnp.bfloat16)
        return _

    lax.fori_loop(0, MAXB, body, 0, unroll=4)

    row_iota = lax.broadcasted_iota(jnp.int32, (ROWS, LANES), 0)
    lane_iota = lax.broadcasted_iota(jnp.int32, (ROWS, LANES), 1)

    def picked_body(index, _):
        picked = jnp.zeros((ROWS, LANES), jnp.float32)
        for row in range(ROWS):
            token = index * ROWS + row
            near_copy(token).wait()
            hit = (row_iota == row) & (lane_iota == ids_ref[token] - place_ref[token] * LANES)
            picked = jnp.where(hit, near[token].astype(jnp.float32), picked)
        picked_ref[rows_of(index), :] = spread(jnp.sum(picked, axis=1, keepdims=True))
        return _

    lax.fori_loop(0, tokens // ROWS, picked_body, 0)

    def wait_seen(slot, _):
        seen_copy(slot).wait()
        return _

    lax.fori_loop(0, MAXB, wait_seen, 0, unroll=8)


def loss_kernel(
    count, sides_ref, picks_ref, blocks_ref, seen_ref, picked_ref, student_ref,
    target_ref, shift_ref, loss_ref,
    logits, top_at, total_at, own_sums, sums, picks, blocks, load_sem, send_sem, recv_sem,
):
    me = lax.axis_index("vocab")
    tokens, width = logits.shape
    per = MAXB // count
    others = [lax.rem(me + step, count) for step in range(1, count)]
    slots = lambda owner: pl.ds(owner * per, per)

    def load(index):
        return pltpu.make_async_copy(
            student_ref.at[rows_of(index)], logits.at[rows_of(index)], load_sem.at[index]
        )

    for index in range(tokens // ROWS):
        load(index).start()
    barrier = greet(others)
    for slot in range(per):
        blocks[me * per + slot] = blocks_ref[me * per + slot]
        picks[me * per + slot] = picks_ref[me * per + slot]
    pl.semaphore_wait(barrier, count - 1)
    copies = []
    for step, other in enumerate(others):
        for kind, source, buffer in ((0, picks_ref, picks), (1, blocks_ref, blocks)):
            copies.append(
                remote(
                    source.at[slots(other)], buffer.at[slots(me)],
                    send_sem.at[kind, step], recv_sem.at[kind, me], other,
                )
            )
    for copy in copies:
        copy.start()

    def student_body(index, _):
        load(index).wait()
        here = rows_of(index)
        top, total = row_stats(lambda start, size: logits[here, pl.ds(start, size)], width)
        top_at[here, :] = spread(top)
        total_at[here, :] = spread(total)
        return _

    lax.fori_loop(0, tokens // ROWS, student_body, 0)

    for step, other in enumerate(others):
        for kind, source, buffer in ((0, picks_ref, picks), (1, blocks_ref, blocks)):
            remote(
                source.at[slots(other)], buffer.at[slots(other)],
                send_sem.at[kind, step], recv_sem.at[kind, other], other,
            ).wait_recv()

    left = lax.broadcasted_iota(jnp.int32, (1, LANES), 1) < BLK

    def target_body(slot, carry):
        mass, cross = carry
        packed = blocks[slot].astype(jnp.float32)
        turned = pltpu.roll(packed, BLK, 1)
        block = jnp.concatenate(
            [jnp.where(left, packed, turned), jnp.where(left, turned, packed)], axis=0
        ).astype(jnp.bfloat16)
        term = lax.dot_general(
            picks[slot], block, (((0,), (0,)), ((), ())), preferred_element_type=jnp.float32
        )
        term = term * sides_ref[pl.ds(slot, 1), :]
        target_ref[slot] = term
        return mass + term, cross + term * seen_ref[slot].astype(jnp.float32)

    zero = jnp.zeros((tokens, LANES), jnp.float32)
    mass, cross = lax.fori_loop(0, MAXB, target_body, (zero, zero), unroll=2)
    sub_iota = lax.broadcasted_iota(jnp.int32, (8, LANES), 0)
    flip = lambda part: jnp.transpose(part)[:8]
    mine = jnp.where(sub_iota == 0, flip(top_at[...]), 0.0)
    mine = jnp.where(sub_iota == 1, flip(total_at[...]), mine)
    mine = jnp.where(sub_iota == 2, flip(picked_ref[...]), mine)
    mine = jnp.where(sub_iota == 3, flip(spread(jnp.sum(mass, axis=1, keepdims=True))), mine)
    mine = jnp.where(sub_iota == 4, flip(spread(jnp.sum(cross, axis=1, keepdims=True))), mine)
    own_sums[...] = mine
    sums[me] = mine
    for step, other in enumerate(others):
        copy = remote(own_sums, sums.at[me], send_sem.at[2, step], recv_sem.at[2, me], other)
        copy.start()
        copies.append(copy)
    for step, other in enumerate(others):
        remote(own_sums, sums.at[other], send_sem.at[2, step], recv_sem.at[2, other], other).wait_recv()
    parts = [sums[index] for index in range(count)]
    top = functools.reduce(jnp.maximum, [part[0:1] for part in parts])
    total = sum(part[1:2] * jnp.exp(part[0:1] - top) for part in parts)
    added = sum(parts)
    log_norm = top + jnp.log(total)
    weight = added[3:4] + 1.0
    loss = weight * log_norm - added[4:5] - added[2:3]
    loss_ref[...] = jnp.broadcast_to(loss, (8, LANES))
    shift_ref[...] = jnp.transpose(jnp.broadcast_to(log_norm - jnp.log(weight), (tokens, LANES)))
    for copy in copies:
        copy.wait_send()


def grad_kernel(tile_ref, first_ref, place_ref, ids_ref, shift_ref, target_ref, logits_ref, grad_ref, merged):
    width = logits_ref.shape[1]
    step = pl.program_id(0)
    shift = shift_ref[...]
    ids = ids_ref[...]

    @pl.when(step == 0)
    def _():
        merged[...] = jnp.zeros_like(merged)

        def body(slot, _):
            first = first_ref[slot]
            merged[first] = merged[first] + target_ref[slot]
            return _

        lax.fori_loop(0, MAXB, body, 0)

    def store(starts, parts):
        for start, part in zip(starts, parts):
            grad_ref[:, pl.ds(start, LANES)] = part.astype(jnp.bfloat16)

    def plain(start):
        return jnp.exp(logits_ref[:, pl.ds(start, LANES)].astype(jnp.float32) - shift)

    def body(index, _):
        starts = [pl.multiple_of(index * CHUNK + k, LANES) for k in range(0, CHUNK, LANES)]
        store(starts, [plain(start).astype(jnp.bfloat16) for start in starts])
        return _

    whole = width // CHUNK
    lax.fori_loop(0, whole, body, 0)
    starts = list(range(whole * CHUNK, width, LANES))
    store(starts, [plain(start) for start in starts])

    lane_iota = lax.broadcasted_iota(jnp.int32, (ROWS, LANES), 1)

    def marked(start):
        return plain(start) - jnp.where(lane_iota + start == ids, 1.0, 0.0)

    tiles = [place_ref[step * ROWS + row] for row in range(ROWS)]
    starts = [pl.multiple_of(tile * LANES, LANES) for tile in tiles]
    store(starts, [marked(start).astype(jnp.bfloat16) for start in starts])
    here = pl.ds(pl.multiple_of(step * ROWS, ROWS), ROWS)
    for begin in range(0, MAXB, 16):
        slots = range(begin, begin + 16)
        starts = [pl.multiple_of(tile_ref[slot] * LANES, LANES) for slot in slots]
        parts = [
            (marked(start) - merged[first_ref[slot], here, :]).astype(jnp.bfloat16)
            for slot, start in zip(slots, starts)
        ]
        store(starts, parts)


def params():
    return pltpu.CompilerParams(vmem_limit_bytes=LIMIT)


def local(
    teacher_logits, student_logits, token_ids, align_values, block_rows, block_cols, block_counts
):
    count = lax.axis_size("vocab")
    me = lax.axis_index("vocab")
    rows = teacher_logits.shape[0]
    width = student_logits.shape[1]
    padded = pl.cdiv(width, LANES) * LANES
    per_dest = MAXB // count
    steps = rows // ROWS
    smem = pl.BlockSpec(memory_space=SMEM)
    vmem = pl.BlockSpec(memory_space=VMEM)
    f32 = lambda *shape: jax.ShapeDtypeStruct(shape, jnp.float32)
    b16 = lambda *shape: jax.ShapeDtypeStruct(shape, jnp.bfloat16)

    live = lax.iota(jnp.int32, MAXB) < block_counts[0]
    sent_blocks = jnp.where(live[:, None], align_values, jnp.zeros_like(align_values))
    sent_blocks = sent_blocks.reshape(MAXB, 2, BLK // 2, BLK).transpose(0, 2, 1, 3)
    sent_blocks = sent_blocks.reshape(MAXB, BLK // 2, LANES)
    own_cols = jnp.broadcast_to(jnp.pad(block_cols, (0, LANES - MAXB))[None, :], (8, LANES))
    ids = token_ids - me * width
    size = rows * width
    dma = pltpu.SemaphoreType.DMA

    def comm_params(number):
        return pltpu.CompilerParams(
            vmem_limit_bytes=LIMIT, collective_id=number, has_side_effects=True
        )

    any_spec = pl.BlockSpec(memory_space=pl.ANY)
    stats, all_cols = pl.pallas_call(
        functools.partial(teacher_kernel, count),
        out_shape=(f32(8, LANES), jax.ShapeDtypeStruct((count, 8, LANES), jnp.int32)),
        in_specs=[vmem, vmem],
        out_specs=(vmem, vmem),
        scratch_shapes=[
            VMEM((rows, LANES), jnp.float32),
            VMEM((rows, LANES), jnp.float32),
            VMEM((8, LANES), jnp.float32),
            VMEM((count, 8, LANES), jnp.float32),
            VMEM((count, 8, LANES), jnp.int32),
            dma((2, count)),
            dma((2, count)),
        ],
        compiler_params=comm_params(1),
    )(own_cols, teacher_logits)

    cols = all_cols[:, 0, :MAXB].reshape(count, count, per_dest)
    cols = lax.dynamic_index_in_dim(cols, me, 1, keepdims=False).reshape(MAXB)
    tile = cols // 2
    first = jnp.argmax(tile[:, None] == tile[None, :], axis=1).astype(jnp.int32)
    place = jnp.clip(ids, 0, width - 1) // LANES
    sides = (lax.iota(jnp.int32, LANES)[None, :] // BLK == (cols % 2)[:, None]).astype(jnp.float32)

    whole_tiles = student_logits
    if padded != width:
        whole_tiles = jnp.pad(student_logits, ((0, 0), (0, padded - width)))
    picks, seen, picked = pl.pallas_call(
        pick_kernel,
        out_shape=(b16(MAXB, BLK, rows), b16(MAXB, rows, LANES), f32(rows, LANES)),
        in_specs=[smem, smem, smem, smem, vmem, vmem, any_spec],
        out_specs=(vmem, vmem, vmem),
        scratch_shapes=[VMEM((rows, ROWS, LANES), jnp.bfloat16), dma((MAXB,)), dma((rows,))],
        compiler_params=params(),
    )(block_rows, tile, ids, place, teacher_logits, stats, whole_tiles)

    target, shift, loss = pl.pallas_call(
        functools.partial(loss_kernel, count),
        out_shape=(f32(MAXB, rows, LANES), f32(rows, LANES), f32(8, LANES)),
        in_specs=[vmem, vmem, vmem, vmem, vmem, any_spec],
        out_specs=(vmem, vmem, vmem),
        scratch_shapes=[
            VMEM((rows, width), jnp.bfloat16),
            VMEM((rows, LANES), jnp.float32),
            VMEM((rows, LANES), jnp.float32),
            VMEM((8, LANES), jnp.float32),
            VMEM((count, 8, LANES), jnp.float32),
            VMEM((MAXB, BLK, rows), jnp.bfloat16),
            VMEM((MAXB, BLK // 2, LANES), jnp.bfloat16),
            dma((steps,)),
            dma((3, count)),
            dma((3, count)),
        ],
        compiler_params=comm_params(0),
    )(sides, picks, sent_blocks, seen, picked, student_logits)
    token_loss = loss[0]

    row_spec = pl.BlockSpec((ROWS, 1), lambda i: (i, 0))
    lane_spec = pl.BlockSpec((ROWS, LANES), lambda i: (i, 0))
    wide_spec = pl.BlockSpec((ROWS, padded), lambda i: (i, 0))
    logit_grad = pl.pallas_call(
        grad_kernel,
        out_shape=b16(rows, width),
        grid=(steps,),
        in_specs=[smem, smem, smem, row_spec, lane_spec, vmem, wide_spec],
        out_specs=wide_spec,
        scratch_shapes=[VMEM((MAXB, rows, LANES), jnp.float32)],
        compiler_params=params(),
        cost_estimate=pl.CostEstimate(flops=8 * size, bytes_accessed=4 * size, transcendentals=size),
    )(tile, first, place, ids[:, None], shift, target, student_logits)
    return logit_grad, token_loss


def solution(mesh):
    return jax.shard_map(
        local,
        mesh=mesh,
        in_specs=(
            P(("groups", "tok", "sub"), "vocab"),
            P(("groups", "tok", "sub"), "vocab"),
            P(("groups", "tok", "sub")),
            P("vocab", None),
            P("vocab"),
            P("vocab"),
            P("vocab"),
        ),
        out_specs=(P(("groups", "tok", "sub"), "vocab"), P(("groups", "tok", "sub"))),
        check_vma=False,
    )
```

time: 99 us -> 69.2 us (0.70)
  blocking collectives: 26 us -> 0 us
  starting transfers between devices: 9.79 us -> 0 us
  Pallas kernels: 49.6 us -> 59.1 us
  other arithmetic: 6.29 us -> 2.5 us
  local copies, waits for them, and re-layouts: 4.57 us -> 5.9 us
    pallas_call x3, Pallas kernels: 22.9 us -> 41.7 us  [the longest x1 27.2 us: local(): pl.pallas_call(functools.partial(loss_kernel, count), out_shape=(f32(MAXB...]
    all_gather x1 -> x0, blocking collectives: 13.7 us -> none  [local(): sums = lax.all_gather(sums, 'vocab')]
    unnamed x1 -> x0, blocking collectives: 12.3 us -> none
    all_to_all x2 -> x0, starting transfers between devices: 9.79 us -> none  [the longest x1 6.32 us: local(): lax.all_to_all(sent_blocks, 'vocab', split_axis=0, concat_axis=0, tiled=T...]
    pallas_call x1, Pallas kernels: 26.8 us -> 17.4 us  [local(): pl.pallas_call(grad_kernel, out_shape=b16(rows, width), grid=(steps,), in...]
    all_to_all x1 -> x0, other arithmetic: 1.74 us -> none  [local(): lax.all_to_all(sent_blocks, 'vocab', split_axis=0, concat_axis=0, tiled=T...]
    select_n x1 -> x4, other arithmetic: 0.01 us -> 1.72 us  [the longest x1 1.04 us: local(): jnp.where(live[:, None], align_values, jnp.zeros_like(align_values))]
    reduce_max x3 -> x0, other arithmetic: 1.47 us -> none  [the longest x2 1.45 us: local(): part_top = jnp.max(scores, axis=1)]
  transfers between devices with their start and end apart: 2 -> 0, of which waited for: 0 -> 0; matrix products, arithmetic and copies ran while one was open for 6% -> 0% of each run, Pallas kernels for 19% -> 0%
where the time goes in v2:
time: 69.2 us; the launch traced here: 68.9 us
  Pallas kernels  59.1 us (85%)
  local copies, waits for them, and re-layouts  5.9 us (9%)
  other arithmetic  2.5 us (4%)
  between operations  1.37 us (2%)
    pallas_call x1, Pallas kernels, local(): pl.pallas_call(functools.partial(loss_kernel, count), out_shape=(f32(MAXB...  27.2 us
    pallas_call x1, Pallas kernels, local(): pl.pallas_call(grad_kernel, out_shape=b16(rows, width), grid=(steps,), in...  17.4 us
    pallas_call x1, Pallas kernels, local(): pl.pallas_call(functools.partial(teacher_kernel, count), out_shape=(f32(8...  8.62 us
    pallas_call x1, Pallas kernels, local(): pl.pallas_call(pick_kernel, out_shape=(b16(MAXB, BLK, rows), b16(MAXB, ro...  5.88 us
    unnamed x6, local copies, waits for them, and re-layouts  3.09 us

profile of v2, /device:TPU:0, one launch (start us, length us, event | category | flops | bytes accessed | tf_op | source)
XLA Modules:
  0.0 68.9 jit_solution(1385913884022360044)
XLA Ops:
  1.3 0.7 pad.4
  2.0 0.7 and_select_fusion.2
  2.6 0.0 copy-start
  2.6 1.2 %copy-done = bf16[128,4096]{1,0:T(8,128)(2,1)S(1)} copy-done((bf16[128,4096]{1,0:T(8,128)(2,1)S(1)}, bf16[128,4096]{1,0:T(8,128)(2,1)}, u32[]{:S(2)}) %copy-start) | copy-done | bytes 1048600
  3.9 8.6 %shard_map.86 = (f32[8,128]{1,0:T(8,128)S(1)}, s32[4,8,128]{2,1,0:T(8,128)S(1)}) custom-call(s32[8,128]{1,0:T(8,128)S(1)} %broadcast_in_dim.14.cols_ref, bf16[128,4096]{1,0:T(8,128)(2,1)S(1)} %copy-done), custom_call_target="tpu_custom_call" | custom-call | tf_op jit(solution)/shard_map/pallas_call | solution.py:374
  12.5 0.1 reshape_squeeze.3
  12.6 0.1 reshape.133
  12.7 0.7 %iota_reduce_fusion = (pred[32]{0:T(512)(128)(4,1)}, s32[32]{0:T(128)S(1)}) fusion(s32[32]{0:T(128)S(1)} %get-tuple-element.23.tile_ref), kind=kLoop, calls=%fused_computation.2 | loop fusion | flops 7968 | bytes 288 | tf_op jit(solution)/shard_map/local/reduce | solution.py:394
  13.4 0.1 compare_convert_fusion.sides_ref
  13.5 0.1 copy.12.ids_ref
  13.6 1.0 %broadcast_select_fusion = bf16[32,4096]{1,0:T(8,128)(2,1)S(1)} fusion(bf16[32,4096]{1,0:T(8,128)(2,1)} %param.10, pred[32]{0:T(512)(128)(4,1)S(1)} %iota_compare_fusion), kind=kLoop, calls=%fused_computation.1 | loop fusion | flops 131072 | bytes 524320 | tf_op jit(solution)/shard_map/jit(_where)/select_n | solution.py:360
  14.7 0.5 reshape.134
  15.2 0.5 copy.14
  15.7 0.3 reshape.135.blocks_ref
  16.0 0.0 copy-start.1
  16.0 1.2 %copy-done.1 = bf16[128,4096]{1,0:T(8,128)(2,1)S(1)} copy-done((bf16[128,4096]{1,0:T(8,128)(2,1)S(1)}, bf16[128,4096]{1,0:T(8,128)(2,1)}, u32[]{:S(2)}) %copy-start.1) | copy-done | bytes 1048600
  17.2 0.0 copy-start.2
  17.2 0.7 copy-done.2
  17.9 5.9 %shard_map.87 = (bf16[32,64,128]{2,1,0:T(8,128)(2,1)S(1)}, bf16[32,128,128]{2,1,0:T(8,128)(2,1)S(1)}, f32[128,128]{1,0:T(8,128)S(1)}) custom-call(s32[32]{0:T(128)S(1)} %copy-done.2, s32[32]{0:T(128)S(1)} %get-tuple-element.23.tile_ref, s32[128]{0:T(128)S(1)} %get-tuple-element.21.ids_ref, s32[128]{0:T(128)S(1)} %get-tuple-element.20.place_ref, ...), custom_call_target="tpu_custom_call" | custom-call | tf_op jit(solution)/shard_map/pallas_call | solution.py:401
  23.8 27.2 %shard_map.88 = (f32[32,128,128]{2,1,0:T(8,128)S(1)}, f32[128,128]{1,0:T(8,128)S(1)}, f32[8,128]{1,0:T(8,128)S(1)}) custom-call(f32[32,128]{1,0:T(8,128)S(1)} %compare_convert_fusion.sides_ref, bf16[32,64,128]{2,1,0:T(8,128)(2,1)S(1)} %get-tuple-element.14.picks_ref, bf16[32,32,128]{2,1,0:T(8,128)(2,1)S(1)} %reshape.135.blocks_ref, ...), custom_call_target="tpu_custom_call" | custom-call | tf_op jit(solution)/shard_map/pallas_call | solution.py:410
  50.9 0.5 slice_bitcast_fusion
  51.4 17.4 %shard_map.89 = bf16[128,64000]{1,0:T(8,128)(2,1)} custom-call(s32[32]{0:T(128)S(1)} %get-tuple-element.23.tile_ref, s32[32]{0:T(128)S(1)} %get-tuple-element.12.first_ref, s32[128]{0:T(128)S(1)} %get-tuple-element.20.place_ref, s32[128,1]{1,0:T(8,128)S(1)} %copy.12.ids_ref, f32[128,128]{1,0:T(8,128)S(1)} %get-tuple-element.17.shift_ref, ...), custom_call_target="tpu_custom_call" | custom-call | flops 65536000 | bytes 32768000 | tf_op jit(solution)/shard_map/pallas_call | solution.py:434
  (6 shorter events, 0.1 us)
Async XLA Ops:
  2.6 1.2 %copy-start = (bf16[128,4096]{1,0:T(8,128)(2,1)S(1)}, bf16[128,4096]{1,0:T(8,128)(2,1)}, u32[]{:S(2)}) copy-start(bf16[128,4096]{1,0:T(8,128)(2,1)} %teacher_ref.3) | copy-start | bytes 3145732
  16.0 1.2 %copy-start.1 = (bf16[128,4096]{1,0:T(8,128)(2,1)S(1)}, bf16[128,4096]{1,0:T(8,128)(2,1)}, u32[]{:S(2)}) copy-start(bf16[128,4096]{1,0:T(8,128)(2,1)} %teacher_ref.3) | copy-start | bytes 3145732
  17.2 0.7 copy-start.2

commit v3 on v2

--- a/solution.py
+++ b/solution.py
@@ -11,7 +11,7 @@
 MAXB = 32
 LANES = 128
 ROWS = 16
-CHUNK = 2560
+CHUNK = 12800
 VMEM = pltpu.VMEM
 SMEM = pltpu.SMEM
 LIMIT = 40 * 1024 * 1024
@@ -23,16 +23,18 @@
 
 def fold(value, join):
     parts = [value[:, k : k + LANES] for k in range(0, value.shape[1], LANES)]
-    while len(parts) > 1:
-        parts = [join(*parts[k : k + 2]) if k + 1 < len(parts) else parts[k] for k in range(0, len(parts), 2)]
-    return parts[0]
+    ways = parts[:4]
+    for index, part in enumerate(parts[4:]):
+        ways[index % 4] = join(ways[index % 4], part)
+    return functools.reduce(join, ways)
 
 
 def row_stats(load, width):
-    whole, tail = divmod(width, CHUNK)
+    step = min(CHUNK, width // LANES * LANES)
+    whole, tail = divmod(width, step)
 
     def chunk(index):
-        return load(pl.multiple_of(index * CHUNK, CHUNK), CHUNK)
+        return load(pl.multiple_of(index * step, LANES), step)
 
     def max_body(index, top):
         return jnp.maximum(top, fold(chunk(index), jnp.maximum))
@@ -41,7 +43,7 @@
     top = lax.fori_loop(0, whole, max_body, top).astype(jnp.float32)
     top = jnp.max(top, axis=1, keepdims=True)
     if tail:
-        rest = load(whole * CHUNK, tail).astype(jnp.float32)
+        rest = load(whole * step, tail).astype(jnp.float32)
         top = jnp.maximum(top, jnp.max(rest, axis=1, keepdims=True))
 
     def sum_body(index, total):
@@ -84,36 +86,47 @@
 
 def teacher_kernel(
     count, cols_ref, teacher_ref, stats_ref, all_cols_ref,
-    top_at, total_at, own_stats, stats, cols, send_sem, recv_sem,
+    logits, top_at, total_at, own_stats, stats, own_cols, cols, load_sem, send_sem, recv_sem,
 ):
     me = lax.axis_index("vocab")
     others = [lax.rem(me + step, count) for step in range(1, count)]
+
+    def load(index):
+        return pltpu.make_async_copy(
+            teacher_ref.at[rows_of(index)], logits.at[rows_of(index)], load_sem.at[index]
+        )
+
+    for index in range(logits.shape[0] // ROWS):
+        load(index).start()
     barrier = greet(others)
+    spare = jnp.zeros((1, LANES - MAXB), jnp.int32)
+    own_cols[...] = jnp.broadcast_to(jnp.concatenate([cols_ref[...], spare], axis=1), (8, LANES))
 
     def body(index, _):
+        load(index).wait()
         here = rows_of(index)
-        top, total = row_stats(lambda start, size: teacher_ref[here, pl.ds(start, size)], teacher_ref.shape[1])
+        top, total = row_stats(lambda start, size: logits[here, pl.ds(start, size)], logits.shape[1])
         top_at[here, :] = spread(top)
         total_at[here, :] = spread(total)
         return _
 
-    lax.fori_loop(0, teacher_ref.shape[0] // ROWS, body, 0)
+    lax.fori_loop(0, logits.shape[0] // ROWS, body, 0)
     sub_iota = lax.broadcasted_iota(jnp.int32, (8, LANES), 0)
     own_stats[...] = jnp.where(
         sub_iota == 0, jnp.transpose(top_at[...])[:8], jnp.transpose(total_at[...])[:8]
     )
     stats[me] = own_stats[...]
-    cols[me] = cols_ref[...]
+    cols[me] = own_cols[...]
     pl.semaphore_wait(barrier, count - 1)
     copies = []
     for step, other in enumerate(others):
         copies.append(remote(own_stats, stats.at[me], send_sem.at[0, step], recv_sem.at[0, me], other))
-        copies.append(remote(cols_ref, cols.at[me], send_sem.at[1, step], recv_sem.at[1, me], other))
+        copies.append(remote(own_cols, cols.at[me], send_sem.at[1, step], recv_sem.at[1, me], other))
     for copy in copies:
         copy.start()
     for step, other in enumerate(others):
         remote(own_stats, stats.at[other], send_sem.at[0, step], recv_sem.at[0, other], other).wait_recv()
-        remote(cols_ref, cols.at[other], send_sem.at[1, step], recv_sem.at[1, other], other).wait_recv()
+        remote(own_cols, cols.at[other], send_sem.at[1, step], recv_sem.at[1, other], other).wait_recv()
     tops = [stats[index, 0:1] for index in range(count)]
     totals = [stats[index, 1:2] for index in range(count)]
     top = functools.reduce(jnp.maximum, tops)
@@ -125,10 +138,13 @@
 
 
 def pick_kernel(
-    rows_ref, tile_ref, ids_ref, place_ref, teacher_ref, stats_ref, student_ref,
-    picks_ref, seen_ref, picked_ref, near, seen_sem, near_sem,
+    rows_ref, count_ref, tile_ref, ids_ref, place_ref, align_ref, teacher_ref, stats_ref, student_ref,
+    picks_ref, blocks_ref, seen_ref, picked_ref,
+    teacher, near, turned, packed, teacher_sem, seen_sem, near_sem,
 ):
     tokens = teacher_ref.shape[0]
+    teacher_copy = pltpu.make_async_copy(teacher_ref, teacher, teacher_sem)
+    teacher_copy.start()
 
     def near_copy(token):
         return pltpu.make_async_copy(
@@ -152,14 +168,25 @@
 
     lax.fori_loop(0, tokens, start_near, 0, unroll=8)
     lax.fori_loop(0, MAXB, start_seen, 0, unroll=8)
+    live = lax.broadcasted_iota(jnp.int32, (MAXB, LANES), 0) < count_ref[0]
+    lines = BLK * BLK // LANES
+    for line in range(lines):
+        part = align_ref[:, line * LANES : (line + 1) * LANES].astype(jnp.float32)
+        packed[pl.ds(line, MAXB, stride=lines), :] = jnp.where(live, part, 0.0)
+    for slot in range(MAXB):
+        blocks_ref[slot] = packed[slot * lines : (slot + 1) * lines, :].astype(jnp.bfloat16)
     top = stats_ref[0:1]
     total = stats_ref[1:2]
+    teacher_copy.wait()
 
     def body(slot, _):
         row = rows_ref[slot]
-        scores = jnp.transpose(teacher_ref[:, lane_tile(row // 2)].astype(jnp.float32))
+        scores = jnp.transpose(teacher[:, lane_tile(row // 2)].astype(jnp.float32))
         scores = jnp.where(row % 2 == 0, scores[:BLK], scores[BLK:])
-        picks_ref[slot] = (jnp.exp(scores - top) / total).astype(jnp.bfloat16)
+        turned[slot] = jnp.exp(scores - top) / total
+        even = turned[slot, pl.ds(0, BLK // 2, stride=2), :]
+        odd = turned[slot, pl.ds(1, BLK // 2, stride=2), :]
+        picks_ref[slot] = jnp.concatenate([even, odd], axis=0).astype(jnp.bfloat16)
         return _
 
     lax.fori_loop(0, MAXB, body, 0, unroll=4)
@@ -255,7 +282,7 @@
         return mass + term, cross + term * seen_ref[slot].astype(jnp.float32)
 
     zero = jnp.zeros((tokens, LANES), jnp.float32)
-    mass, cross = lax.fori_loop(0, MAXB, target_body, (zero, zero), unroll=2)
+    mass, cross = lax.fori_loop(0, MAXB, target_body, (zero, zero), unroll=4)
     sub_iota = lax.broadcasted_iota(jnp.int32, (8, LANES), 0)
     flip = lambda part: jnp.transpose(part)[:8]
     mine = jnp.where(sub_iota == 0, flip(top_at[...]), 0.0)
@@ -278,7 +305,7 @@
     log_norm = top + jnp.log(total)
     weight = added[3:4] + 1.0
     loss = weight * log_norm - added[4:5] - added[2:3]
-    loss_ref[...] = jnp.broadcast_to(loss, (8, LANES))
+    loss_ref[...] = loss
     shift_ref[...] = jnp.transpose(jnp.broadcast_to(log_norm - jnp.log(weight), (tokens, LANES)))
     for copy in copies:
         copy.wait_send()
@@ -356,11 +383,6 @@
     f32 = lambda *shape: jax.ShapeDtypeStruct(shape, jnp.float32)
     b16 = lambda *shape: jax.ShapeDtypeStruct(shape, jnp.bfloat16)
 
-    live = lax.iota(jnp.int32, MAXB) < block_counts[0]
-    sent_blocks = jnp.where(live[:, None], align_values, jnp.zeros_like(align_values))
-    sent_blocks = sent_blocks.reshape(MAXB, 2, BLK // 2, BLK).transpose(0, 2, 1, 3)
-    sent_blocks = sent_blocks.reshape(MAXB, BLK // 2, LANES)
-    own_cols = jnp.broadcast_to(jnp.pad(block_cols, (0, LANES - MAXB))[None, :], (8, LANES))
     ids = token_ids - me * width
     size = rows * width
     dma = pltpu.SemaphoreType.DMA
@@ -374,19 +396,22 @@
     stats, all_cols = pl.pallas_call(
         functools.partial(teacher_kernel, count),
         out_shape=(f32(8, LANES), jax.ShapeDtypeStruct((count, 8, LANES), jnp.int32)),
-        in_specs=[vmem, vmem],
+        in_specs=[vmem, any_spec],
         out_specs=(vmem, vmem),
         scratch_shapes=[
+            VMEM(teacher_logits.shape, jnp.bfloat16),
             VMEM((rows, LANES), jnp.float32),
             VMEM((rows, LANES), jnp.float32),
             VMEM((8, LANES), jnp.float32),
             VMEM((count, 8, LANES), jnp.float32),
+            VMEM((8, LANES), jnp.int32),
             VMEM((count, 8, LANES), jnp.int32),
+            dma((steps,)),
             dma((2, count)),
             dma((2, count)),
         ],
         compiler_params=comm_params(1),
-    )(own_cols, teacher_logits)
+    )(block_cols[None, :], teacher_logits)
 
     cols = all_cols[:, 0, :MAXB].reshape(count, count, per_dest)
     cols = lax.dynamic_index_in_dim(cols, me, 1, keepdims=False).reshape(MAXB)
@@ -398,18 +423,31 @@
     whole_tiles = student_logits
     if padded != width:
         whole_tiles = jnp.pad(student_logits, ((0, 0), (0, padded - width)))
-    picks, seen, picked = pl.pallas_call(
+    picks, sent_blocks, seen, picked = pl.pallas_call(
         pick_kernel,
-        out_shape=(b16(MAXB, BLK, rows), b16(MAXB, rows, LANES), f32(rows, LANES)),
-        in_specs=[smem, smem, smem, smem, vmem, vmem, any_spec],
-        out_specs=(vmem, vmem, vmem),
-        scratch_shapes=[VMEM((rows, ROWS, LANES), jnp.bfloat16), dma((MAXB,)), dma((rows,))],
+        out_shape=(
+            b16(MAXB, BLK, rows),
+            b16(MAXB, BLK // 2, LANES),
+            b16(MAXB, rows, LANES),
+            f32(rows, LANES),
+        ),
+        in_specs=[smem, smem, smem, smem, smem, vmem, any_spec, vmem, any_spec],
+        out_specs=(vmem, vmem, vmem, vmem),
+        scratch_shapes=[
+            VMEM(teacher_logits.shape, jnp.bfloat16),
+            VMEM((rows, ROWS, LANES), jnp.bfloat16),
+            VMEM((MAXB, BLK, rows), jnp.float32),
+            VMEM((MAXB * BLK // 2, LANES), jnp.float32),
+            dma,
+            dma((MAXB,)),
+            dma((rows,)),
+        ],
         compiler_params=params(),
-    )(block_rows, tile, ids, place, teacher_logits, stats, whole_tiles)
+    )(block_rows, block_counts, tile, ids, place, align_values, teacher_logits, stats, whole_tiles)
 
     target, shift, loss = pl.pallas_call(
         functools.partial(loss_kernel, count),
-        out_shape=(f32(MAXB, rows, LANES), f32(rows, LANES), f32(8, LANES)),
+        out_shape=(f32(MAXB, rows, LANES), f32(rows, LANES), f32(1, LANES)),
         in_specs=[vmem, vmem, vmem, vmem, vmem, any_spec],
         out_specs=(vmem, vmem, vmem),
         scratch_shapes=[
@@ -426,7 +464,7 @@
         ],
         compiler_params=comm_params(0),
     )(sides, picks, sent_blocks, seen, picked, student_logits)
-    token_loss = loss[0]
+    token_loss = loss.reshape(rows)
 
     row_spec = pl.BlockSpec((ROWS, 1), lambda i: (i, 0))
     lane_spec = pl.BlockSpec((ROWS, LANES), lambda i: (i, 0))

time: 69.2 us -> 68.5 us (0.990)
  other arithmetic: 2.5 us -> 1.46 us
  Pallas kernels: 59.1 us -> 59.8 us
    unnamed x6 -> x11, local copies, waits for them, and re-layouts: 3.09 us -> 5.21 us
    pallas_call x1, Pallas kernels: 27.2 us -> 25.6 us  [local(): pl.pallas_call(functools.partial(loss_kernel, count), out_shape=(f32(MAXB...]
    pallas_call x1, Pallas kernels: 8.62 us -> 10 us  [local(): pl.pallas_call(functools.partial(teacher_kernel, count), out_shape=(f32(8...]
    reshape x3 -> x0, local copies, waits for them, and re-layouts: 1.3 us -> none  [the longest x2 1.04 us: local(): sent_blocks.reshape(MAXB, 2, BLK // 2, BLK).transpose(0, 2, 1, 3)]
    select_n x1 -> x0, other arithmetic: 1.04 us -> none  [local(): jnp.where(live[:, None], align_values, jnp.zeros_like(align_values))]
where the time goes in v3:
time: 68.5 us; the launch traced here: 68.2 us
  Pallas kernels  59.8 us (87%)
  local copies, waits for them, and re-layouts  5.54 us (8%)
  other arithmetic  1.46 us (2%)
  between operations  1.34 us (2%)
    pallas_call x1, Pallas kernels, local(): pl.pallas_call(functools.partial(loss_kernel, count), out_shape=(f32(MAXB...  25.6 us
    pallas_call x1, Pallas kernels, local(): pl.pallas_call(grad_kernel, out_shape=b16(rows, width), grid=(steps,), in...  17.6 us
    pallas_call x1, Pallas kernels, local(): pl.pallas_call(functools.partial(teacher_kernel, count), out_shape=(f32(8...  10 us
    pallas_call x1, Pallas kernels, local(): pl.pallas_call(pick_kernel, out_shape=(b16(MAXB, BLK, rows), b16(MAXB, BL...  6.56 us
    unnamed x11, local copies, waits for them, and re-layouts  5.21 us

profile of v3, /device:TPU:0, one launch (start us, length us, event | category | flops | bytes accessed | tf_op | source)
XLA Modules:
  0.0 68.2 jit_solution(17901237783017539669)
XLA Ops:
  1.3 0.7 and_select_fusion.2
  2.0 0.0 copy-start
  2.0 1.2 %copy-done = bf16[128,4096]{1,0:T(8,128)(2,1)S(1)} copy-done((bf16[128,4096]{1,0:T(8,128)(2,1)S(1)}, bf16[128,4096]{1,0:T(8,128)(2,1)}, u32[]{:S(2)}) %copy-start) | copy-done | bytes 1048600
  3.2 0.0 copy-start.3
  3.2 0.7 copy-done.3
  3.8 10.0 %shard_map.86 = (f32[8,128]{1,0:T(8,128)S(1)}, s32[4,8,128]{2,1,0:T(8,128)S(1)}) custom-call(s32[1,32]{1,0:T(1,128)S(1)} %bitcast.4, bf16[128,4096]{1,0:T(8,128)(2,1)S(1)} %copy-done), custom_call_target="tpu_custom_call" | custom-call | tf_op jit(solution)/shard_map/pallas_call | solution.py:396
  13.9 0.1 reshape_squeeze.3
  14.0 0.1 reshape.125
  14.1 0.7 %iota_reduce_fusion = (pred[32]{0:T(512)(128)(4,1)}, s32[32]{0:T(128)S(1)}) fusion(s32[32]{0:T(128)S(1)} %get-tuple-element.25.tile_ref), kind=kLoop, calls=%fused_computation | loop fusion | flops 7968 | bytes 288 | tf_op jit(solution)/shard_map/local/reduce | solution.py:419
  14.8 0.1 compare_convert_fusion.sides_ref
  14.9 0.1 copy.10.ids_ref
  15.0 0.0 copy-start.1
  15.0 1.2 %copy-done.1 = bf16[128,4096]{1,0:T(8,128)(2,1)S(1)} copy-done((bf16[128,4096]{1,0:T(8,128)(2,1)S(1)}, bf16[128,4096]{1,0:T(8,128)(2,1)}, u32[]{:S(2)}) %copy-start.1) | copy-done | bytes 1048600
  16.2 0.0 copy-start.2
  16.2 0.9 %copy-done.2 = bf16[32,4096]{1,0:T(8,128)(2,1)S(1)} copy-done((bf16[32,4096]{1,0:T(8,128)(2,1)S(1)}, bf16[32,4096]{1,0:T(8,128)(2,1)}, u32[]{:S(2)}) %copy-start.2) | copy-done | bytes 262168
  17.2 0.0 copy-start.4
  17.2 0.7 copy-done.4
  17.8 6.6 %shard_map.87 = (bf16[32,64,128]{2,1,0:T(8,128)(2,1)S(1)}, bf16[32,32,128]{2,1,0:T(8,128)(2,1)S(1)}, bf16[32,128,128]{2,1,0:T(8,128)(2,1)S(1)}, f32[128,128]{1,0:T(8,128)S(1)}) custom-call(s32[32]{0:T(128)S(1)} %copy-done.4, s32[1]{0:T(128)S(6)} %copy.12.count_ref, s32[32]{0:T(128)S(1)} %get-tuple-element.25.tile_ref, s32[128]{0:T(128)S(1)} %get-tuple-element.23.ids_ref, ...), custom_call_target="tpu_custom_call" | custom-call | tf_op jit(solution)/shard_map/pallas_call | solution.py:426
  24.4 25.6 %shard_map.88 = (f32[32,128,128]{2,1,0:T(8,128)S(1)}, f32[128,128]{1,0:T(8,128)S(1)}, f32[1,128]{1,0:T(1,128)S(1)}) custom-call(f32[32,128]{1,0:T(8,128)S(1)} %compare_convert_fusion.sides_ref, bf16[32,64,128]{2,1,0:T(8,128)(2,1)S(1)} %get-tuple-element.15.picks_ref, bf16[32,32,128]{2,1,0:T(8,128)(2,1)S(1)} %get-tuple-element.16.blocks_ref, ...), custom_call_target="tpu_custom_call" | custom-call | tf_op jit(solution)/shard_map/pallas_call | solution.py:448
  50.0 17.6 %shard_map.89 = bf16[128,64000]{1,0:T(8,128)(2,1)} custom-call(s32[32]{0:T(128)S(1)} %get-tuple-element.25.tile_ref, s32[32]{0:T(128)S(1)} %get-tuple-element.13.first_ref, s32[128]{0:T(128)S(1)} %get-tuple-element.22.place_ref, s32[128,1]{1,0:T(8,128)S(1)} %copy.10.ids_ref, f32[128,128]{1,0:T(8,128)S(1)} %get-tuple-element.19.shift_ref, ...), custom_call_target="tpu_custom_call" | custom-call | flops 65536000 | bytes 32768000 | tf_op jit(solution)/shard_map/pallas_call | solution.py:472
  67.6 0.5 copy.13
  (4 shorter events, 0.1 us)
Async XLA Ops:
  2.0 1.2 %copy-start = (bf16[128,4096]{1,0:T(8,128)(2,1)S(1)}, bf16[128,4096]{1,0:T(8,128)(2,1)}, u32[]{:S(2)}) copy-start(bf16[128,4096]{1,0:T(8,128)(2,1)} %teacher_ref.3) | copy-start | bytes 3145732
  3.2 0.7 copy-start.3
  15.0 1.2 %copy-start.1 = (bf16[128,4096]{1,0:T(8,128)(2,1)S(1)}, bf16[128,4096]{1,0:T(8,128)(2,1)}, u32[]{:S(2)}) copy-start(bf16[128,4096]{1,0:T(8,128)(2,1)} %teacher_ref.3) | copy-start | bytes 3145732
  16.2 0.9 %copy-start.2 = (bf16[32,4096]{1,0:T(8,128)(2,1)S(1)}, bf16[32,4096]{1,0:T(8,128)(2,1)}, u32[]{:S(2)}) copy-start(bf16[32,4096]{1,0:T(8,128)(2,1)} %align_ref.1) | copy-start | bytes 786436
  17.2 0.7 copy-start.4

commit v4 on v3

--- a/solution.py
+++ b/solution.py
@@ -11,6 +11,7 @@
 MAXB = 32
 LANES = 128
 ROWS = 16
+EARLY = 3
 CHUNK = 12800
 VMEM = pltpu.VMEM
 SMEM = pltpu.SMEM
@@ -85,8 +86,8 @@
 
 
 def teacher_kernel(
-    count, cols_ref, teacher_ref, stats_ref, all_cols_ref,
-    logits, top_at, total_at, own_stats, stats, own_cols, cols, load_sem, send_sem, recv_sem,
+    count, cols_ref, teacher_ref, student_ref, stats_ref, all_cols_ref, early_top_ref, early_total_ref,
+    logits, student, student_sem, top_at, total_at, own_stats, stats, own_cols, cols, load_sem, send_sem, recv_sem,
 ):
     me = lax.axis_index("vocab")
     others = [lax.rem(me + step, count) for step in range(1, count)]
@@ -96,8 +97,15 @@
             teacher_ref.at[rows_of(index)], logits.at[rows_of(index)], load_sem.at[index]
         )
 
+    def load_student(index):
+        return pltpu.make_async_copy(
+            student_ref.at[rows_of(index)], student.at[rows_of(index)], student_sem.at[index]
+        )
+
     for index in range(logits.shape[0] // ROWS):
         load(index).start()
+    for index in range(EARLY):
+        load_student(index).start()
     barrier = greet(others)
     spare = jnp.zeros((1, LANES - MAXB), jnp.int32)
     own_cols[...] = jnp.broadcast_to(jnp.concatenate([cols_ref[...], spare], axis=1), (8, LANES))
@@ -124,6 +132,16 @@
         copies.append(remote(own_cols, cols.at[me], send_sem.at[1, step], recv_sem.at[1, me], other))
     for copy in copies:
         copy.start()
+
+    def student_body(index, _):
+        load_student(index).wait()
+        here = rows_of(index)
+        top, total = row_stats(lambda start, size: student[here, pl.ds(start, size)], student.shape[1])
+        early_top_ref[here, :] = spread(top)
+        early_total_ref[here, :] = spread(total)
+        return _
+
+    lax.fori_loop(0, EARLY, student_body, 0)
     for step, other in enumerate(others):
         remote(own_stats, stats.at[other], send_sem.at[0, step], recv_sem.at[0, other], other).wait_recv()
         remote(own_cols, cols.at[other], send_sem.at[1, step], recv_sem.at[1, other], other).wait_recv()
@@ -214,7 +232,7 @@
 
 
 def loss_kernel(
-    count, sides_ref, picks_ref, blocks_ref, seen_ref, picked_ref, student_ref,
+    count, sides_ref, picks_ref, blocks_ref, seen_ref, picked_ref, early_top_ref, early_total_ref, student_ref,
     target_ref, shift_ref, loss_ref,
     logits, top_at, total_at, own_sums, sums, picks, blocks, load_sem, send_sem, recv_sem,
 ):
@@ -229,9 +247,11 @@
             student_ref.at[rows_of(index)], logits.at[rows_of(index)], load_sem.at[index]
         )
 
-    for index in range(tokens // ROWS):
+    for index in range(EARLY, tokens // ROWS):
         load(index).start()
     barrier = greet(others)
+    top_at[: EARLY * ROWS, :] = early_top_ref[...]
+    total_at[: EARLY * ROWS, :] = early_total_ref[...]
     for slot in range(per):
         blocks[me * per + slot] = blocks_ref[me * per + slot]
         picks[me * per + slot] = picks_ref[me * per + slot]
@@ -256,7 +276,7 @@
         total_at[here, :] = spread(total)
         return _
 
-    lax.fori_loop(0, tokens // ROWS, student_body, 0)
+    lax.fori_loop(EARLY, tokens // ROWS, student_body, 0)
 
     for step, other in enumerate(others):
         for kind, source, buffer in ((0, picks_ref, picks), (1, blocks_ref, blocks)):
@@ -393,13 +413,20 @@
         )
 
     any_spec = pl.BlockSpec(memory_space=pl.ANY)
-    stats, all_cols = pl.pallas_call(
+    stats, all_cols, early_top, early_total = pl.pallas_call(
         functools.partial(teacher_kernel, count),
-        out_shape=(f32(8, LANES), jax.ShapeDtypeStruct((count, 8, LANES), jnp.int32)),
-        in_specs=[vmem, any_spec],
-        out_specs=(vmem, vmem),
+        out_shape=(
+            f32(8, LANES),
+            jax.ShapeDtypeStruct((count, 8, LANES), jnp.int32),
+            f32(EARLY * ROWS, LANES),
+            f32(EARLY * ROWS, LANES),
+        ),
+        in_specs=[vmem, any_spec, any_spec],
+        out_specs=(vmem, vmem, vmem, vmem),
         scratch_shapes=[
             VMEM(teacher_logits.shape, jnp.bfloat16),
+            VMEM((EARLY * ROWS, width), jnp.bfloat16),
+            dma((EARLY,)),
             VMEM((rows, LANES), jnp.float32),
             VMEM((rows, LANES), jnp.float32),
             VMEM((8, LANES), jnp.float32),
@@ -411,7 +438,7 @@
             dma((2, count)),
         ],
         compiler_params=comm_params(1),
-    )(block_cols[None, :], teacher_logits)
+    )(block_cols[None, :], teacher_logits, student_logits)
 
     cols = all_cols[:, 0, :MAXB].reshape(count, count, per_dest)
     cols = lax.dynamic_index_in_dim(cols, me, 1, keepdims=False).reshape(MAXB)
@@ -448,7 +475,7 @@
     target, shift, loss = pl.pallas_call(
         functools.partial(loss_kernel, count),
         out_shape=(f32(MAXB, rows, LANES), f32(rows, LANES), f32(1, LANES)),
-        in_specs=[vmem, vmem, vmem, vmem, vmem, any_spec],
+        in_specs=[vmem, vmem, vmem, vmem, vmem, vmem, vmem, any_spec],
         out_specs=(vmem, vmem, vmem),
         scratch_shapes=[
             VMEM((rows, width), jnp.bfloat16),
@@ -463,7 +490,7 @@
             dma((3, count)),
         ],
         compiler_params=comm_params(0),
-    )(sides, picks, sent_blocks, seen, picked, student_logits)
+    )(sides, picks, sent_blocks, seen, picked, early_top, early_total, student_logits)
     token_loss = loss.reshape(rows)
 
     row_spec = pl.BlockSpec((ROWS, 1), lambda i: (i, 0))

time: 68.5 us -> 66.8 us (0.975)
  local copies, waits for them, and re-layouts: 5.54 us -> 2.73 us
  Pallas kernels: 59.8 us -> 61 us
    unnamed x11, local copies, waits for them, and re-layouts: 5.21 us -> 2.4 us
    pallas_call x1, Pallas kernels: 25.6 us -> 26.3 us  [local(): pl.pallas_call(functools.partial(loss_kernel, count), out_shape=(f32(MAXB...]
where the time goes in v4:
time: 66.8 us; the launch traced here: 66.5 us
  Pallas kernels  61 us (91%)
  local copies, waits for them, and re-layouts  2.73 us (4%)
  other arithmetic  1.46 us (2%)
  between operations  1.35 us (2%)
    pallas_call x1, Pallas kernels, local(): pl.pallas_call(functools.partial(loss_kernel, count), out_shape=(f32(MAXB...  26.3 us
    pallas_call x1, Pallas kernels, local(): pl.pallas_call(grad_kernel, out_shape=b16(rows, width), grid=(steps,), in...  17.6 us
    pallas_call x1, Pallas kernels, local(): pl.pallas_call(functools.partial(teacher_kernel, count), out_shape=(f32(8...  10.5 us
    pallas_call x1, Pallas kernels, local(): pl.pallas_call(pick_kernel, out_shape=(b16(MAXB, BLK, rows), b16(MAXB, BL...  6.56 us
    unnamed x11, local copies, waits for them, and re-layouts  2.4 us

profile of v4, /device:TPU:0, one launch (start us, length us, event | category | flops | bytes accessed | tf_op | source)
XLA Modules:
  0.0 66.5 jit_solution(14978436053849443100)
XLA Ops:
  0.6 0.0 copy-start.4
  1.3 0.7 %and_select_fusion.2 = (s32[128]{0:T(128)S(1)}, s32[128]{0:T(128)S(1)}) fusion(s32[128]{0:T(128)} %param.9, s32[]{:T(128)S(6)} %mul.3), kind=kLoop, calls=%fused_computation.6 | loop fusion | flops 2176 | bytes 1540 | tf_op jit(solution)/shard_map/jit(floor_divide)/jit(_where)/select_n | solution.py:447
  2.0 0.1 copy.10.ids_ref
  2.1 0.0 copy-start
  2.1 1.2 %copy-done = bf16[128,4096]{1,0:T(8,128)(2,1)S(1)} copy-done((bf16[128,4096]{1,0:T(8,128)(2,1)S(1)}, bf16[128,4096]{1,0:T(8,128)(2,1)}, u32[]{:S(2)}) %copy-start) | copy-done | bytes 1048600
  3.3 0.0 copy-start.3
  3.3 0.7 copy-done.3
  4.0 0.0 copy-start.1
  4.0 0.0 copy-start.2
  4.0 10.5 %shard_map.86 = (f32[8,128]{1,0:T(8,128)S(1)}, s32[4,8,128]{2,1,0:T(8,128)S(1)}, f32[48,128]{1,0:T(8,128)S(1)}, f32[48,128]{1,0:T(8,128)S(1)}) custom-call(s32[1,32]{1,0:T(1,128)S(1)} %bitcast.4, bf16[128,4096]{1,0:T(8,128)(2,1)S(1)} %copy-done, bf16[128,64000]{1,0:T(8,128)(2,1)} %logits_ref.1), custom_call_target="tpu_custom_call" | custom-call | tf_op jit(solution)/shard_map/pallas_call | solution.py:416
  14.5 0.1 reshape_squeeze.3
  14.6 0.1 reshape.125
  14.7 0.7 %iota_reduce_fusion = (pred[32]{0:T(512)(128)(4,1)}, s32[32]{0:T(128)S(1)}) fusion(s32[32]{0:T(128)S(1)} %get-tuple-element.29.tile_ref), kind=kLoop, calls=%fused_computation | loop fusion | flops 7968 | bytes 288 | tf_op jit(solution)/shard_map/local/reduce | solution.py:446
  15.4 0.1 compare_convert_fusion.sides_ref
  15.5 0.0 copy-done.4
  15.5 0.0 copy-done.1
  15.5 0.0 copy-done.2
  15.5 6.6 %shard_map.87 = (bf16[32,64,128]{2,1,0:T(8,128)(2,1)S(1)}, bf16[32,32,128]{2,1,0:T(8,128)(2,1)S(1)}, bf16[32,128,128]{2,1,0:T(8,128)(2,1)S(1)}, f32[128,128]{1,0:T(8,128)S(1)}) custom-call(s32[32]{0:T(128)S(1)} %copy-done.4, s32[1]{0:T(128)S(6)} %copy.12.count_ref, s32[32]{0:T(128)S(1)} %get-tuple-element.29.tile_ref, s32[128]{0:T(128)S(1)} %get-tuple-element.27.ids_ref, ...), custom_call_target="tpu_custom_call" | custom-call | tf_op jit(solution)/shard_map/pallas_call | solution.py:453
  22.0 26.3 %shard_map.88 = (f32[32,128,128]{2,1,0:T(8,128)S(1)}, f32[128,128]{1,0:T(8,128)S(1)}, f32[1,128]{1,0:T(1,128)S(1)}) custom-call(f32[32,128]{1,0:T(8,128)S(1)} %compare_convert_fusion.sides_ref, bf16[32,64,128]{2,1,0:T(8,128)(2,1)S(1)} %get-tuple-element.17.picks_ref, bf16[32,32,128]{2,1,0:T(8,128)(2,1)S(1)} %get-tuple-element.18.blocks_ref, ...), custom_call_target="tpu_custom_call" | custom-call | tf_op jit(solution)/shard_map/pallas_call | solution.py:475
  48.4 17.6 %shard_map.89 = bf16[128,64000]{1,0:T(8,128)(2,1)} custom-call(s32[32]{0:T(128)S(1)} %get-tuple-element.29.tile_ref, s32[32]{0:T(128)S(1)} %get-tuple-element.15.first_ref, s32[128]{0:T(128)S(1)} %get-tuple-element.26.place_ref, s32[128,1]{1,0:T(8,128)S(1)} %copy.10.ids_ref, f32[128,128]{1,0:T(8,128)S(1)} %get-tuple-element.23.shift_ref, ...), custom_call_target="tpu_custom_call" | custom-call | flops 65536000 | bytes 32768000 | tf_op jit(solution)/shard_map/pallas_call | solution.py:499
  66.0 0.5 copy.13
  (4 shorter events, 0.1 us)
Async XLA Ops:
  0.6 14.8 %copy-start.4 = (s32[32]{0:T(128)S(1)}, s32[32]{0:T(128)}, u32[]{:S(2)}) copy-start(s32[32]{0:T(128)} %rows_ref.1) | copy-start | bytes 388
  2.1 1.2 %copy-start = (bf16[128,4096]{1,0:T(8,128)(2,1)S(1)}, bf16[128,4096]{1,0:T(8,128)(2,1)}, u32[]{:S(2)}) copy-start(bf16[128,4096]{1,0:T(8,128)(2,1)} %teacher_ref.3) | copy-start | bytes 3145732
  3.3 0.7 copy-start.3
  4.0 11.5 %copy-start.1 = (bf16[128,4096]{1,0:T(8,128)(2,1)S(1)}, bf16[128,4096]{1,0:T(8,128)(2,1)}, u32[]{:S(2)}) copy-start(bf16[128,4096]{1,0:T(8,128)(2,1)} %teacher_ref.3) | copy-start | bytes 3145732
  4.0 11.5 %copy-start.2 = (bf16[32,4096]{1,0:T(8,128)(2,1)S(1)}, bf16[32,4096]{1,0:T(8,128)(2,1)}, u32[]{:S(2)}) copy-start(bf16[32,4096]{1,0:T(8,128)(2,1)} %align_ref.1) | copy-start | bytes 786436
